TPU v7x, 32 devices: a whole 2x2x4 slice. The times are simulated.
32 devices in a mesh: gx: 8 (over z, core), gy: 4 (over y, x).
Axes of the slice: x: 2, y: 2, z: 4, core: 2. Of those that a mesh axis runs over, the one named last changes fastest.
Arguments:
- features: bfloat16 [8, 4, 32, 64, 256], P('gx', 'gy'), may hold values from -6 to 6
- weights: bfloat16 [27, 256, 256], replicated, may hold values from -0.078125 to 0.078125
- cotangent: bfloat16 [8, 4, 32, 64, 256], P('gx', 'gy'), may hold values from -6 to 6
- send_lists: int32 [8, 4, 8, 8], P('gx', 'gy'), may hold values from 0 to 31, as said below
- block_offset: int32 [8, 4, 108], P('gx', 'gy'), may hold values from 0 to 26, as said below
- block_input: int32 [8, 4, 108, 8], P('gx', 'gy'), may hold values from 0 to 95
- block_output: int32 [8, 4, 108, 8], P('gx', 'gy'), may hold values from 0 to 32, as said below
- block_count: int32 [8, 4], P('gx', 'gy'), may hold values from 1 to 108, as said below
Outputs:
- out_features: bfloat16 [8, 4, 32, 64, 256], P('gx', 'gy')
- feat_grad: bfloat16 [8, 4, 32, 64, 256], P('gx', 'gy')
- weight_grad: float32 [27, 256, 256], replicated
Inputs may be any that keep to these rules, and one draw needn't show every extreme that they name: `send_lists`: each of a device's 8 lists names 8 different tiles that the device holds. `block_offset`: 0 in blocks past block_count. `block_output`: 32 marks an unused pair; a device's used pairs of one offset name different tiles; the used blocks come first, grouped by offset, and blocks past block_count hold only unused pairs. `block_count`: some device uses all 108 blocks.
All inputs are finite; a program needn't handle non-finite values.
Results may differ from a plain program's by a relative error of at most 0.0029.
Values may be sent and summed in bfloat16 or wider, within the bound.
No kernel may reach another device: no remote copies, remote signals or barrier semaphores. Data moves between devices by JAX's collectives and lax.ppermute only.
A program may use at most 128 MiB of HBM per device.

v0:
```python
import math

import jax
import jax.numpy as jnp
from jax import lax
from jax.experimental import pallas as pl
from jax.experimental.pallas import tpu as pltpu
from jax.sharding import Mesh
from jax.sharding import PartitionSpec as P

DIRECTIONS = ((-1, -1), (-1, 0), (-1, 1), (0, -1), (0, 1), (1, -1), (1, 0), (1, 1))
BUNDLES = (
    ((0, -1),),
    ((0, 1),),
    ((-1, -1), (1, -1)),
    ((-1, 1), (1, 1)),
    ((-1, 0),),
    ((1, 0),),
)
MIB = 1024 * 1024
ANY = pl.BlockSpec(memory_space=pl.ANY)
HBM = pl.BlockSpec(memory_space=pltpu.HBM)
VMEM = pl.BlockSpec(memory_space=pltpu.VMEM)
SMEM = pl.BlockSpec(memory_space=pltpu.SMEM)


def chunk_of(size, wanted):
    return max(c for c in range(1, wanted + 1) if size % c == 0)


def x_size():
    return lax.axis_size("gz") * lax.axis_size("core")


def travel(packet, step_x, step_y):
    size_x, size_y = x_size(), lax.axis_size("gy")
    pairs = [
        (i * size_y + j, (i + step_x) * size_y + j + step_y)
        for i in range(size_x)
        for j in range(size_y)
        if 0 <= i + step_x < size_x and 0 <= j + step_y < size_y
    ]
    return lax.ppermute(packet, ("gz", "core", "gy"), pairs)


def pack(tiles, lists):
    halo = lists.shape[1]
    _, voxels, channels = tiles.shape

    def kernel(lists_ref, tiles_ref, *packets):
        for d, packet in enumerate(packets):
            for h in range(halo):
                packet[h] = tiles_ref[lists_ref[d, h]]

    return pl.pallas_call(
        kernel,
        out_shape=[jax.ShapeDtypeStruct((halo, voxels, channels), tiles.dtype)] * len(DIRECTIONS),
        in_specs=[SMEM, VMEM],
        out_specs=[VMEM] * len(DIRECTIONS),
        compiler_params=pltpu.CompilerParams(vmem_limit_bytes=16 * MIB),
        name="pack",
    )(lists, tiles)


def source_table(offsets, inputs, outputs, count, offset_count, tile_slots, empty, after):
    rows, blocks = inputs.shape

    def kernel(offsets_ref, inputs_ref, outputs_ref, count_ref, _, table_ref):
        def clear(k, carry):
            for t in range(tile_slots):
                table_ref[k, t] = empty
            return carry

        lax.fori_loop(0, offset_count, clear, 0)

        def block(n, carry):
            k = offsets_ref[n]
            for q in range(rows):
                table_ref[k, outputs_ref[q, n]] = inputs_ref[q, n]
            return carry

        lax.fori_loop(0, jnp.minimum(count_ref[0], blocks), block, 0)

    return pl.pallas_call(
        kernel,
        out_shape=jax.ShapeDtypeStruct((offset_count, tile_slots + 1), jnp.int32),
        in_specs=[SMEM] * 4 + [ANY],
        out_specs=SMEM,
        cost_estimate=pl.CostEstimate(flops=4 * 10**9, bytes_accessed=MIB, transcendentals=0),
        name="source_table",
    )(offsets, inputs, outputs, count, after)


def gathered(table_ref, ext, k, first, count):
    return jnp.concatenate([ext[table_ref[k, first + t]] for t in range(count)], axis=0)


def write_half(table_ref, late, ext, turned_ref, out_ref, out_hbm, sem, scale):
    offset_count, part, _ = out_ref.shape
    tile_slots = table_ref.shape[1] - 1
    count = (offset_count + 1) // 2

    def turn(j, carry):
        k = late * (offset_count - count) + j
        terms = jnp.dot(
            turned_ref[...],
            gathered(table_ref, ext, k, 0, tile_slots),
            preferred_element_type=jnp.float32,
        )
        terms = terms.T * scale
        for b in range(2):
            place = 2 * k + b - late * offset_count

            @pl.when((place >= 0) & (place < offset_count))
            def _():
                out_ref[place] = terms[b * part : (b + 1) * part]
                pltpu.make_async_copy(out_ref.at[place], out_hbm.at[place], sem).start()

        return carry

    lax.fori_loop(0, count, turn, 0)
    pltpu.make_async_copy(out_ref, out_hbm, sem).wait()


def turn_weights(weights, after):
    def kernel(_, w_ref, out_ref):
        for k in range(w_ref.shape[0]):
            out_ref[k] = w_ref[k].astype(jnp.float32).T.astype(out_ref.dtype)

    offset_count, channels, _ = weights.shape
    step = chunk_of(offset_count, 3)
    spec = pl.BlockSpec((step, channels, channels), lambda k: (k, 0, 0))
    return pl.pallas_call(
        kernel,
        grid=(offset_count // step,),
        out_shape=jax.ShapeDtypeStruct(weights.shape, weights.dtype),
        in_specs=[SMEM, spec],
        out_specs=spec,
        compiler_params=pltpu.CompilerParams(vmem_limit_bytes=16 * MIB),
        cost_estimate=pl.CostEstimate(flops=8 * 10**9, bytes_accessed=7 * MIB, transcendentals=0),
        name="turn_weights",
    )(after, weights)


def forward_and_terms(table, half, tiles, halos, weights, cotangent, scale, after):
    tile_slots, voxels, channels = tiles.shape
    offset_count = weights.shape[0]
    directions, halo = len(halos), halos[0].shape[0]
    empty = tile_slots + directions * halo
    group = chunk_of(tile_slots, 8)
    groups = tile_slots // group
    rows = group * voxels
    deep = chunk_of(offset_count, 9)

    def kernel(table_ref, half_ref, tiles_ref, *refs):
        halo_refs, refs = refs[:directions], refs[directions:]
        w_hbm, cot_hbm, _, out_hbm, grad_hbm, turned_hbm, ext_hbm, half_hbm = refs[:8]
        w_ref, cot_ref, out_ref, grad, turned_ref, ext, half_out, acc, sems, w_sems = refs[8:]
        copies = [pltpu.make_async_copy(tiles_ref, ext.at[pl.ds(0, tile_slots)], sems.at[0])]
        for d, halo_ref in enumerate(halo_refs):
            place = ext.at[pl.ds(tile_slots + d * halo, halo)]
            copies.append(pltpu.make_async_copy(halo_ref, place, sems.at[d + 6]))

        def load_mats(step):
            part = pl.ds(step * deep, deep)
            return pltpu.make_async_copy(w_hbm.at[part], w_ref.at[part], w_sems.at[step])

        load_cot = pltpu.make_async_copy(cot_hbm, cot_ref, sems.at[1])
        for copy in copies + [load_mats(n) for n in range(offset_count // deep)] + [load_cot]:
            copy.start()
        ext[empty] = jnp.zeros((voxels, channels), ext.dtype)
        acc[...] = jnp.zeros_like(acc)
        for copy in copies:
            copy.wait()
        saves = [pltpu.make_async_copy(ext, ext_hbm, sems.at[2])]
        saves[0].start()

        def turn(step, carry):
            load_mats(step).wait()
            mats = w_ref[pl.ds(step * deep, deep)].reshape(deep * channels, channels)
            for g in range(groups):
                lhs = jnp.concatenate(
                    [
                        gathered(table_ref, ext, step * deep + j, g * group, group)
                        for j in range(deep)
                    ],
                    axis=1,
                )
                acc[g] += jnp.dot(lhs, mats, preferred_element_type=jnp.float32)
            return carry

        lax.fori_loop(0, offset_count // deep, turn, 0)
        load_cot.wait()

        def finish(t, carry):
            pre = acc[t // group, pl.ds(pl.multiple_of((t % group) * voxels, voxels), voxels), :]
            sigma = jax.nn.sigmoid(pre)
            out_ref[t] = (ext[t].astype(jnp.float32) + pre * sigma).astype(out_ref.dtype)
            incoming = cot_ref[t].astype(jnp.float32)
            grad[t] = (incoming * sigma * (1.0 + pre * (1.0 - sigma))).astype(grad.dtype)
            return carry

        lax.fori_loop(0, tile_slots, finish, 0)
        for g in range(groups):
            part = grad[pl.ds(g * group, group)].reshape(rows, channels)
            turned_ref[:, pl.ds(g * rows, rows)] = part.astype(jnp.float32).T.astype(jnp.bfloat16)
        saves += [
            pltpu.make_async_copy(out_ref, out_hbm, sems.at[3]),
            pltpu.make_async_copy(grad, grad_hbm, sems.at[4]),
            pltpu.make_async_copy(turned_ref, turned_hbm, sems.at[5]),
        ]
        for save in saves[1:]:
            save.start()
        write_half(
            table_ref, half_ref[0], ext, turned_ref, half_out, half_hbm, sems.at[directions + 6], scale
        )
        for save in saves:
            save.wait()

    flops = 3 * offset_count * tile_slots * voxels * channels * channels
    out_shape = [
        jax.ShapeDtypeStruct(tiles.shape, jnp.bfloat16),
        jax.ShapeDtypeStruct(tiles.shape, jnp.bfloat16),
        jax.ShapeDtypeStruct((channels, tile_slots * voxels), jnp.bfloat16),
        jax.ShapeDtypeStruct((empty + 1, voxels, channels), jnp.bfloat16),
        jax.ShapeDtypeStruct((offset_count, channels // 2, channels), jnp.float32),
    ]
    return pl.pallas_call(
        kernel,
        out_shape=out_shape,
        in_specs=[SMEM, SMEM, HBM] + [ANY] * directions + [HBM, HBM, ANY],
        out_specs=[HBM] * 5,
        scratch_shapes=[
            pltpu.VMEM(weights.shape, jnp.bfloat16),
            pltpu.VMEM(tiles.shape, jnp.bfloat16),
        ]
        + [pltpu.VMEM(one.shape, one.dtype) for one in out_shape]
        + [
            pltpu.VMEM((groups, rows, channels), jnp.float32),
            pltpu.SemaphoreType.DMA((directions + 7,)),
            pltpu.SemaphoreType.DMA((offset_count // deep,)),
        ],
        compiler_params=pltpu.CompilerParams(vmem_limit_bytes=60 * MIB),
        cost_estimate=pl.CostEstimate(flops=flops, bytes_accessed=20 * MIB, transcendentals=0),
        name="forward_and_terms",
    )(table, half, tiles, *halos, weights, cotangent, after)


def weight_terms(table, half, ext, turned, offset_count, scale):
    channels = ext.shape[2]

    def kernel(table_ref, half_ref, ext_hbm, turned_hbm, out_hbm, ext_ref, turned_ref, out_ref, sems):
        copies = [pltpu.make_async_copy(turned_hbm, turned_ref, sems.at[0])]
        slots = ext_ref.shape[0]
        for n in range(4):
            part = pl.ds(n * slots // 4, (n + 1) * slots // 4 - n * slots // 4)
            copies.append(pltpu.make_async_copy(ext_hbm.at[part], ext_ref.at[part], sems.at[n + 1]))
        for copy in copies:
            copy.start()
        for copy in copies:
            copy.wait()
        write_half(table_ref, half_ref[0], ext_ref, turned_ref, out_ref, out_hbm, sems.at[5], scale)

    flops = offset_count * turned.shape[1] * channels * channels
    out_shape = jax.ShapeDtypeStruct((offset_count, channels // 2, channels), jnp.float32)
    return pl.pallas_call(
        kernel,
        out_shape=out_shape,
        in_specs=[SMEM, SMEM, HBM, HBM],
        out_specs=HBM,
        scratch_shapes=[
            pltpu.VMEM(ext.shape, ext.dtype),
            pltpu.VMEM(turned.shape, turned.dtype),
            pltpu.VMEM(out_shape.shape, out_shape.dtype),
            pltpu.SemaphoreType.DMA((6,)),
        ],
        compiler_params=pltpu.CompilerParams(vmem_limit_bytes=60 * MIB),
        cost_estimate=pl.CostEstimate(flops=flops, bytes_accessed=6 * MIB, transcendentals=0),
        name="weight_terms",
    )(table, half, ext, turned)


def input_grad(table, pre_grad, turned_weights, halo):
    tile_slots, voxels, channels = pre_grad.shape
    offset_count = turned_weights.shape[0]
    empty = tile_slots + len(DIRECTIONS) * halo
    group = chunk_of(tile_slots, 8)
    groups = tile_slots // group
    rows = group * voxels
    unroll = chunk_of(offset_count, 3)
    bundles = len(BUNDLES)

    def kernel(table_ref, grad_hbm, w_hbm, own_hbm, *refs):
        adjoints_hbm, refs = refs[:bundles], refs[bundles:]
        own_ref, adjoints, refs = refs[0], refs[1 : bundles + 1], refs[bundles + 1 :]
        even, odd, grad, w_ref, sems = refs
        copies = [
            pltpu.make_async_copy(grad_hbm, grad, sems.at[0]),
            pltpu.make_async_copy(w_hbm, w_ref, sems.at[1]),
        ]
        for copy in copies:
            copy.start()
        for one in (even, odd):
            one[...] = jnp.zeros_like(one)
        for copy in copies:
            copy.wait()

        def turn(step, carry):
            for j in range(unroll):
                k = step * unroll + j
                for g in range(groups):
                    back = jnp.dot(
                        grad[pl.ds(g * group, group)].reshape(rows, channels),
                        w_ref[k],
                        preferred_element_type=jnp.float32,
                    )
                    for t in range(group):
                        slot = table_ref[k, g * group + t]
                        sums = (even, odd)[t % 2]
                        sums[slot] += back[t * voxels : (t + 1) * voxels]
            return carry

        lax.fori_loop(0, offset_count // unroll, turn, 0)

        saves = []
        for n, (bundle, adjoint) in enumerate(zip(BUNDLES, adjoints)):
            for m, pair in enumerate(bundle):
                for h in range(halo):
                    slot = tile_slots + DIRECTIONS.index(pair) * halo + h
                    adjoint[m * halo + h] = (even[slot] + odd[slot]).astype(jnp.bfloat16)
            saves.append(pltpu.make_async_copy(adjoint, adjoints_hbm[n], sems.at[n + 2]))
            saves[-1].start()

        def own(t, carry):
            own_ref[t] = even[t] + odd[t]
            return carry

        half = tile_slots // 2
        for n in range(2):
            lax.fori_loop(n * half, (n + 1) * half, own, 0)
            part = pl.ds(n * half, half)
            saves.append(
                pltpu.make_async_copy(own_ref.at[part], own_hbm.at[part], sems.at[bundles + 2 + n])
            )
            saves[-1].start()
        for save in saves:
            save.wait()

    flops = 2 * offset_count * tile_slots * voxels * channels * channels
    out_shape = [jax.ShapeDtypeStruct(pre_grad.shape, jnp.float32)] + [
        jax.ShapeDtypeStruct((len(bundle) * halo, voxels, channels), jnp.bfloat16)
        for bundle in BUNDLES
    ]
    return pl.pallas_call(
        kernel,
        out_shape=out_shape,
        in_specs=[SMEM, HBM, HBM],
        out_specs=[HBM] * (bundles + 1),
        scratch_shapes=[pltpu.VMEM(one.shape, one.dtype) for one in out_shape]
        + [pltpu.VMEM((empty + 1, voxels, channels), jnp.float32)] * 2
        + [
            pltpu.VMEM(pre_grad.shape, jnp.bfloat16),
            pltpu.VMEM(turned_weights.shape, jnp.bfloat16),
            pltpu.SemaphoreType.DMA((bundles + 4,)),
        ],
        compiler_params=pltpu.CompilerParams(vmem_limit_bytes=60 * MIB),
        cost_estimate=pl.CostEstimate(flops=flops, bytes_accessed=12 * MIB, transcendentals=0),
        name="input_grad",
    )(table, pre_grad, turned_weights)


def to_other_core(x):
    return lax.ppermute(x, "core", [(0, 1), (1, 0)])


def ring(axis):
    size = lax.axis_size(axis)

    def move(x, by):
        return lax.ppermute(x, axis, [(i, (i + by) % size) for i in range(size)])

    return size, lax.axis_index(axis), move


def given_out(terms, ring):
    size, place, _ = ring
    parts = []
    for s in range(size):
        blocks = [
            lax.dynamic_index_in_dim(
                one.reshape(size, one.shape[0] // size, one.shape[1]), (place + s) % size, keepdims=False
            )
            for one in terms
        ]
        parts.append(sum(blocks[1:], blocks[0]))
    return parts[0], [one.astype(jnp.bfloat16) for one in parts[1:]]


def handed(parts, ring):
    return [ring[2](one, s + 1) for s, one in enumerate(parts)]


def added(mine, arrived):
    for one in arrived:
        mine = mine + one.astype(jnp.float32)
    return mine


def fetched(piece, ring):
    return [ring[2](piece, -s) for s in range(1, ring[0])]


def in_order(piece, others, ring):
    size, place, _ = ring
    whole = jnp.zeros((size,) + piece.shape, piece.dtype)
    for s, one in enumerate([piece, *others]):
        whole = lax.dynamic_update_index_in_dim(whole, one, (place + s) % size, 0)
    return whole.reshape(size * piece.shape[0], piece.shape[1])


def together(*values):
    return lax.optimization_barrier(values)


def widen(place, half, whole):
    rows, channels = half.shape
    turns = chunk_of(rows // 16, 3)
    step = rows // turns

    def kernel(place_ref, half_ref, *refs):
        refs[-1][...] = half_ref[...].astype(jnp.float32)

    given = [] if whole is None else [whole]
    return pl.pallas_call(
        kernel,
        grid_spec=pltpu.PrefetchScalarGridSpec(
            num_scalar_prefetch=1,
            grid=(turns,),
            in_specs=[pl.BlockSpec((step, channels), lambda i, place: (i, 0))] + [ANY] * len(given),
            out_specs=pl.BlockSpec((step, channels), lambda i, place: (place[0] * turns + i, 0)),
        ),
        out_shape=jax.ShapeDtypeStruct((2 * rows, channels), jnp.float32),
        input_output_aliases={2: 0} if given else {},
        compiler_params=pltpu.CompilerParams(vmem_limit_bytes=24 * MIB),
        name="widen",
    )(place, half, *given)


def combine(lists, own, cotangent, returned):
    halo = lists.shape[1]
    tile_slots = own.shape[0]
    arrays = [array for array, _ in returned]

    def kernel(lists_ref, own_ref, cot_ref, *refs):
        out_ref, acc = refs[len(arrays) :]

        def start(t, carry):
            acc[t] = own_ref[t] + cot_ref[t].astype(jnp.float32)
            return carry

        lax.fori_loop(0, tile_slots, start, 0)
        for ref, (_, pairs) in zip(refs, returned):
            for n, pair in enumerate(pairs):
                for h in range(halo):
                    tile = lists_ref[DIRECTIONS.index(pair), h]
                    acc[tile] += ref[n * halo + h].astype(jnp.float32)

        def finish(t, carry):
            out_ref[t] = acc[t].astype(out_ref.dtype)
            return carry

        lax.fori_loop(0, tile_slots, finish, 0)

    return pl.pallas_call(
        kernel,
        out_shape=jax.ShapeDtypeStruct(own.shape, jnp.bfloat16),
        in_specs=[SMEM] + [VMEM] * (len(arrays) + 2),
        out_specs=VMEM,
        scratch_shapes=[pltpu.VMEM(own.shape, jnp.float32)],
        compiler_params=pltpu.CompilerParams(vmem_limit_bytes=16 * MIB),
        name="combine",
    )(lists, own, cotangent, *arrays)


def shards(
    features, weights, cotangent, send_lists, block_offset, block_input, block_output, block_count
):
    tiles = features[0, 0]
    incoming = cotangent[0, 0]
    lists = send_lists[0, 0]
    tile_slots, voxels, channels = tiles.shape
    directions, halo = lists.shape
    device_total = x_size() * lax.axis_size("gy")
    scale = 1.0 / math.sqrt(voxels * tile_slots * device_total)
    offset_count = weights.shape[0]
    core = lax.axis_index("core").astype(jnp.int32)[None]

    packets = pack(tiles, lists)
    table = source_table(
        block_offset[0, 0],
        block_input[0, 0].T,
        block_output[0, 0].T,
        block_count[0],
        offset_count,
        tile_slots,
        tile_slots + directions * halo,
        packets[0],
    )
    turned_weights = turn_weights(weights, table)
    order = [
        DIRECTIONS.index(pair)
        for pair in ((-1, -1), (1, 1), (-1, 0), (1, 0), (-1, 1), (1, -1), (0, -1), (0, 1))
    ]
    arrived = {d: travel(packets[d], *DIRECTIONS[d]) for d in order}
    halos = [arrived[d] for d in range(directions)]
    out_features, pre_grad, turned, ext, send = forward_and_terms(
        table, 1 - core, tiles, halos, weights, incoming, scale, turned_weights
    )
    received = to_other_core(send)
    keep = weight_terms(table, core, ext, turned, offset_count, scale)
    levels = ring("gy"), ring("gz")
    mine, out = given_out([keep.reshape(-1, channels), received.reshape(-1, channels)], levels[0])

    pre_grad, *out = together(pre_grad, *out)
    moved = handed(out, levels[0])
    own, low, high, low_both, high_both, behind, ahead = input_grad(table, pre_grad, turned_weights, halo)
    low, high = travel(low, 0, 1), travel(high, 0, -1)
    low, high, *moved = together(low, high, *moved)
    low_both, high_both = travel(low_both, 0, 1), travel(high_both, 0, -1)

    mine, out = given_out([added(mine, moved)], levels[1])
    piece = added(mine, handed(out, levels[1])).astype(jnp.bfloat16)
    low_both, piece = together(low_both, piece)
    piece = in_order(piece, fetched(piece, levels[1]), levels[1])
    high_both, piece = together(high_both, piece)
    behind = jnp.concatenate([behind, low_both[:halo], high_both[:halo]])
    ahead = jnp.concatenate([ahead, low_both[halo:], high_both[halo:]])
    behind, ahead = travel(behind, 1, 0), travel(ahead, -1, 0)
    own_half = in_order(piece, fetched(piece, levels[0]), levels[0])
    behind, ahead, own_half = together(behind, ahead, own_half)
    feat_grad = combine(
        lists,
        own,
        incoming,
        [
            (low, ((0, -1),)),
            (high, ((0, 1),)),
            (behind, ((-1, 0), (-1, -1), (-1, 1))),
            (ahead, ((1, 0), (1, -1), (1, 1))),
        ],
    )
    other_half = to_other_core(own_half)
    weight_grad = widen(1 - core, other_half, widen(core, own_half, None)).reshape(weights.shape)
    return (out_features[None, None], feat_grad[None, None], weight_grad)


def solution(mesh):
    size_x, size_y = mesh.devices.shape
    split = Mesh(mesh.devices.reshape(size_x // 2, 2, size_y), ("gz", "core", "gy"))
    place = P(("gz", "core"), "gy")
    return jax.shard_map(
        shards,
        mesh=split,
        in_specs=(place, P(), place, place, place, place, place, place),
        out_specs=(place, place, P()),
        check_vma=False,
    )
```

profile of v0, /device:TPU:0, one launch (start us, length us, event | category | flops | bytes accessed | tf_op | source)
XLA Modules:
  0.0 165.6 jit_solution(10488134883756306262)
XLA Ops:
  0.6 0.0 copy-start.1
  0.6 1.2 copy-done.1
  1.9 0.7 copy-done.3
  2.5 1.7 %pack.1 = (bf16[8,64,256]{2,1,0:T(8,128)(2,1)}, bf16[8,64,256]{2,1,0:T(8,128)(2,1)}, bf16[8,64,256]{2,1,0:T(8,128)(2,1)}, bf16[8,64,256]{2,1,0:T(8,128)(2,1)}, b...) custom-call(s32[8,8]{1,0:T(8,128)S(1)} %bitcast.69, ...), custom_call_target="tpu_custom_call" | custom-call | tf_op jit(solution)/shard_map/pack/pallas_call | solution.py:55
  4.3 1.3 collective-permute-start
  5.6 1.3 collective-permute-start.1
  6.9 1.4 collective-permute-start.2
  8.3 1.3 collective-permute-start.3
  9.6 6.1 %collective-permute-start.4 = (bf16[8,64,256]{2,1,0:T(8,128)(2,1)}, bf16[8,64,256]{2,1,0:T(8,128)(2,1)}, u32[]{:S(2)}, u32[]{:S(2)}) collective-permute-start(bf16[8,64,256]{2,1,0:T(8,128)(2,1)} %get-tuple-element.43), channel_id=1, source_target_pairs={{0,1},{1,2},{2,3},{4,5},{5,6},{6,7},{8,9},{9,10},{10,11},{12,13},{... | collective-permute-start | bytes 786440 | tf_op jit(solution)/shard_map/ppermute | solution.py:43
  16.4 0.0 copy-start.5
  16.4 3.1 %source_table.1._.table_ref = s32[27,33]{1,0:T(8,128)} custom-call(s32[108]{0:T(128)} %bitcast.85, s32[8,108]{1,0:T(8,128)} %bitcast.83, s32[8,108]{1,0:T(8,128)} %bitcast.84, s32[1]{0:T(128)} %bitcast.62.count_ref, bf16[8,64,256]{2,1,0:T(8,128)(2,1)} %get-tuple-element.39._), custom_call_target="tpu_custom_call" | custom-call | flops 4000000000 | bytes 1048576 | tf_op jit(solution)/shard_map/source_table/pallas_call | solution.py:84
  19.4 0.0 collective-permute-done.refs_0_
  19.5 1.4 collective-permute-start.5
  20.9 0.0 collective-permute-done.1.refs_1_
  20.9 5.3 %collective-permute-start.6 = (bf16[8,64,256]{2,1,0:T(8,128)(2,1)}, bf16[8,64,256]{2,1,0:T(8,128)(2,1)}, u32[]{:S(2)}, u32[]{:S(2)}) collective-permute-start(bf16[8,64,256]{2,1,0:T(8,128)(2,1)} %copy-done.7), channel_id=1, source_target_pairs={{0,4},{1,5},{2,6},{3,7},{4,8},{5,9},{6,10},{7,11},{8,12},{9,13},{1... | collective-permute-start | bytes 786440 | tf_op jit(solution)/shard_map/ppermute | solution.py:43
  26.1 0.0 collective-permute-done.2.refs_2_
  26.1 9.9 %collective-permute-start.7 = (bf16[8,64,256]{2,1,0:T(8,128)(2,1)}, bf16[8,64,256]{2,1,0:T(8,128)(2,1)}, u32[]{:S(2)}, u32[]{:S(2)}) collective-permute-start(bf16[8,64,256]{2,1,0:T(8,128)(2,1)} %copy-done.6), channel_id=1, source_target_pairs={{0,5},{1,6},{2,7},{4,9},{5,10},{6,11},{8,13},{9,14},{10,15},{12,17... | collective-permute-start | bytes 786440 | tf_op jit(solution)/shard_map/ppermute | solution.py:43
  36.0 0.7 copy-done.10
  36.7 2.5 %turn_weights.1.refs_10_.w_hbm = bf16[27,256,256]{2,1,0:T(8,128)(2,1)S(1)} custom-call(s32[27,33]{1,0:T(8,128)S(1)} %copy-done.10, bf16[27,256,256]{2,1,0:T(8,128)(2,1)S(1)} %copy-done.5), custom_call_target="tpu_custom_call" | custom-call | flops 8000000000 | bytes 7340032 | tf_op jit(solution)/shard_map/turn_weights/pallas_call | solution.py:133
  39.2 0.0 copy-start.9
  39.2 1.8 %copy-done.9 = bf16[27,256,256]{2,1,0:T(8,128)(2,1)} copy-done((bf16[27,256,256]{2,1,0:T(8,128)(2,1)}, bf16[27,256,256]{2,1,0:T(8,128)(2,1)S(1)}, u32[]{:S(2)}) %copy-start.9) | copy-done | bytes 3538968
  41.0 0.0 collective-permute-done.3.refs_3_
  41.0 20.8 %forward_and_terms.1 = (bf16[32,64,256]{2,1,0:T(8,128)(2,1)}, bf16[32,64,256]{2,1,0:T(8,128)(2,1)}, bf16[256,2048]{1,0:T(8,128)(2,1)}, bf16[97,64,256]{2,1,0:T(8,128)(2,1)}, f32[27,128,256]{2,1,0:T(8,128)}) custom-call(s32[27,33]{1,0:T(8,128)} %source_table.1._.table_ref, s32[1]{0:T(128)S(6)} %sub.4.half_ref.place_ref, bf16[32,64,256]{2,1,0:T(8,128)(2,1)} %bitcast.65, ...), custom_call_target="tpu_custom_call" | custom-call | flops 10871635968 | bytes 20971520 | tf_op jit(solution)/shard_map/forward_and_terms/pallas_call | solution.py:228
  61.8 0.1 collective-permute-start.8
  62.0 11.2 %weight_terms.1 = f32[27,128,256]{2,1,0:T(8,128)} custom-call(s32[27,33]{1,0:T(8,128)} %source_table.1._.table_ref, s32[1]{0:T(128)} %bitcast.8.half_ref.place_ref, bf16[97,64,256]{2,1,0:T(8,128)(2,1)} %get-tuple-element.49.ext_hbm, bf16[256,2048]{1,0:T(8,128)(2,1)} %get-tuple-element.50.turned_hbm), custom_call_target="tpu_custom_call" | custom-call | flops 3623878656 | bytes 6291456 | tf_op jit(solution)/shard_map/weight_terms/pallas_call | solution.py:266
  73.1 4.2 %fusion.4 = (bf16[864,256]{1,0:T(8,128)(2,1)}, bf16[864,256]{1,0:T(8,128)(2,1)}, bf16[864,256]{1,0:T(8,128)(2,1)}) fusion(f32[4,864,256]{2,1,0:T(8,128)S(1)} %bitcast.72, s32[]{:T(128)S(6)} %select_n.104, f32[4,864,256]{2,1,0:T(8,128)} %bitcast.74, s32[]{:T(128)S(6)} %select_n.102, s32[]{:T(128)S(6)} %select_n.100), kind=kLoop, calls=%fused_computation.10 | loop fusion | flops 1327104 | bytes 6635532 | tf_op jit(solution)/shard_map/convert_element_type | solution.py:396
  77.4 2.4 %collective-permute-start.11 = (bf16[864,256]{1,0:T(8,128)(2,1)}, bf16[864,256]{1,0:T(8,128)(2,1)}, u32[]{:S(2)}, u32[]{:S(2)}) collective-permute-start(bf16[864,256]{1,0:T(8,128)(2,1)} %get-tuple-element.56), channel_id=1, source_target_pairs={{0,1},{1,2},{2,3},{3,0},{4,5},{5,6},{6,7},{7,4},{8,9},{9,10},{10,1... | collective-permute-start | bytes 1327112 | tf_op jit(solution)/shard_map/ppermute | solution.py:380
  79.7 0.3 collective-permute-start.12
  80.0 2.7 %collective-permute-start.13 = (bf16[864,256]{1,0:T(8,128)(2,1)}, bf16[864,256]{1,0:T(8,128)(2,1)}, u32[]{:S(2)}, u32[]{:S(2)}) collective-permute-start(bf16[864,256]{1,0:T(8,128)(2,1)} %get-tuple-element.58), channel_id=1, source_target_pairs={{0,3},{1,0},{2,1},{3,2},{4,7},{5,4},{6,5},{7,6},{8,11},{9,8},{10,9... | collective-permute-start | bytes 1327112 | tf_op jit(solution)/shard_map/ppermute | solution.py:380
  82.8 15.5 %input_grad.1 = (f32[32,64,256]{2,1,0:T(8,128)}, bf16[8,64,256]{2,1,0:T(8,128)(2,1)}, bf16[8,64,256]{2,1,0:T(8,128)(2,1)}, bf16[16,64,256]{2,1,0:T(8,128)(2,1)},...) custom-call(s32[27,33]{1,0:T(8,128)} %source_table.1._.table_ref, ...), custom_call_target="tpu_custom_call" | custom-call | flops 7247757312 | bytes 12582912 | tf_op jit(solution)/shard_map/input_grad/pallas_call | solution.py:354
  98.2 1.3 collective-permute-start.9
  99.5 1.3 collective-permute-start.10
  100.9 4.3 %collective-permute-done.9.refs_0_ = bf16[8,64,256]{2,1,0:T(8,128)(2,1)S(1)} collective-permute-done((bf16[8,64,256]{2,1,0:T(8,128)(2,1)}, bf16[8,64,256]{2,1,0:T(8,128)(2,1)S(1)}, u32[]{:S(2)}, u32[]{:S(2)}) %collective-permute-start.9) | collective-permute-done | bytes 262176 | tf_op jit(solution)/shard_map/ppermute | solution.py:43
  105.2 5.5 %collective-permute-start.14 = (bf16[16,64,256]{2,1,0:T(8,128)(2,1)}, bf16[16,64,256]{2,1,0:T(8,128)(2,1)S(1)}, u32[]{:S(2)}, u32[]{:S(2)}) collective-permute-start(bf16[16,64,256]{2,1,0:T(8,128)(2,1)} %get-tuple-element.62), channel_id=1, source_target_pairs={{0,1},{1,2},{2,3},{4,5},{5,6},{6,7},{8,9},{9,10},{10,11},{12,13},{... | collective-permute-start | bytes 1572872 | tf_op jit(solution)/shard_map/ppermute | solution.py:43
  110.7 3.6 %collective-permute-done.10.refs_1_ = bf16[8,64,256]{2,1,0:T(8,128)(2,1)S(1)} collective-permute-done((bf16[8,64,256]{2,1,0:T(8,128)(2,1)}, bf16[8,64,256]{2,1,0:T(8,128)(2,1)S(1)}, u32[]{:S(2)}, u32[]{:S(2)}) %collective-permute-start.10) | collective-permute-done | bytes 262176 | tf_op jit(solution)/shard_map/ppermute | solution.py:43
  114.4 2.1 %fusion.1 = f32[864,256]{1,0:T(8,128)S(1)} fusion(bf16[864,256]{1,0:T(8,128)(2,1)} %collective-permute-done.13, bf16[864,256]{1,0:T(8,128)(2,1)} %collective-permute-done.12, bf16[864,256]{1,0:T(8,128)(2,1)} %collective-permute-done.11, f32[4,864,256]{2,1,0:T(8,128)} %bitcast.73, s32[]{:T(128)S(6)} %select_n.106, f32[4,864,256]{2,1,0:T(8,128)} %bitcast.75), kind=kLoop, calls=%fused_computation.2 | loop fusion | flops 1548288 | bytes 3981316 | tf_op jit(solution)/shard_map/add | solution.py:405
  116.4 0.1 fusion.8
  116.5 3.9 %collective-permute-start.17 = (bf16[216,256]{1,0:T(8,128)(2,1)S(1)}, bf16[216,256]{1,0:T(8,128)(2,1)S(1)}, u32[]{:S(2)}, u32[]{:S(2)}) collective-permute-start(bf16[216,256]{1,0:T(8,128)(2,1)S(1)} %get-tuple-element.79), channel_id=1, source_target_pairs={{0,24},{8,0},{16,8},{24,16},{1,25},{9,1},{17,9},{25,17},{2,26},{10... | collective-permute-start | bytes 331784 | tf_op jit(solution)/shard_map/ppermute | solution.py:380
  120.4 2.2 %collective-permute-start.16 = (bf16[216,256]{1,0:T(8,128)(2,1)S(1)}, bf16[216,256]{1,0:T(8,128)(2,1)S(1)}, u32[]{:S(2)}, u32[]{:S(2)}) collective-permute-start(bf16[216,256]{1,0:T(8,128)(2,1)S(1)} %get-tuple-element.80), channel_id=1, source_target_pairs={{0,16},{8,24},{16,0},{24,8},{1,17},{9,25},{17,1},{25,9},{2,18},{10... | collective-permute-start | bytes 331784 | tf_op jit(solution)/shard_map/ppermute | solution.py:380
  122.6 1.6 collective-permute-start.15
  124.2 1.3 collective-permute-start.18
  125.5 4.6 %collective-permute-done.16 = bf16[216,256]{1,0:T(8,128)(2,1)S(1)} collective-permute-done((bf16[216,256]{1,0:T(8,128)(2,1)S(1)}, bf16[216,256]{1,0:T(8,128)(2,1)S(1)}, u32[]{:S(2)}, u32[]{:S(2)}) %collective-permute-start.16) | collective-permute-done | bytes 110624 | tf_op jit(solution)/shard_map/ppermute | solution.py:380
  130.2 0.1 fusion.7
  130.3 1.1 collective-permute-start.19
  131.4 1.5 collective-permute-start.20
  132.9 1.9 %collective-permute-start.21 = (bf16[216,256]{1,0:T(8,128)(2,1)S(1)}, bf16[216,256]{1,0:T(8,128)(2,1)S(1)}, u32[]{:S(2)}, u32[]{:S(2)}) collective-permute-start(bf16[216,256]{1,0:T(8,128)(2,1)S(1)} %fusion.7), channel_id=1, source_target_pairs={{0,8},{8,16},{16,24},{24,0},{1,9},{9,17},{17,25},{25,1},{2,10},{10... | collective-permute-start | bytes 331784 | tf_op jit(solution)/shard_map/ppermute | solution.py:380
  135.0 1.2 collective-permute-done.19
  136.3 4.0 %collective-permute-done.20 = bf16[216,256]{1,0:T(8,128)(2,1)S(1)} collective-permute-done((bf16[216,256]{1,0:T(8,128)(2,1)S(1)}, bf16[216,256]{1,0:T(8,128)(2,1)S(1)}, u32[]{:S(2)}, u32[]{:S(2)}) %collective-permute-start.20) | collective-permute-done | bytes 110624 | tf_op jit(solution)/shard_map/ppermute | solution.py:380
  140.4 0.1 collective-permute-start.24
  140.4 1.7 %collective-permute-start.25 = (bf16[864,256]{1,0:T(8,128)(2,1)S(1)}, bf16[864,256]{1,0:T(8,128)(2,1)S(1)}, u32[]{:S(2)}, u32[]{:S(2)}) collective-permute-start(bf16[864,256]{1,0:T(8,128)(2,1)S(1)} %bitcast.79), channel_id=1, source_target_pairs={{0,2},{1,3},{2,0},{3,1},{4,6},{5,7},{6,4},{7,5},{8,10},{9,11},{10,... | collective-permute-start | bytes 1327112 | tf_op jit(solution)/shard_map/ppermute | solution.py:380
  142.2 1.0 collective-permute-start.26
  143.2 0.1 pad_maximum_fusion
  143.3 1.3 collective-permute-start.22
  144.7 0.1 pad_maximum_fusion.1
  144.8 1.3 collective-permute-start.23
  146.1 0.1 broadcast_in_dim.48
  146.3 6.2 %collective-permute-done.24 = bf16[864,256]{1,0:T(8,128)(2,1)S(1)} collective-permute-done((bf16[864,256]{1,0:T(8,128)(2,1)S(1)}, bf16[864,256]{1,0:T(8,128)(2,1)S(1)}, u32[]{:S(2)}, u32[]{:S(2)}) %collective-permute-start.24) | collective-permute-done | bytes 442400 | tf_op jit(solution)/shard_map/ppermute | solution.py:380
  152.5 4.8 %collective-permute-done.25 = bf16[864,256]{1,0:T(8,128)(2,1)S(1)} collective-permute-done((bf16[864,256]{1,0:T(8,128)(2,1)S(1)}, bf16[864,256]{1,0:T(8,128)(2,1)S(1)}, u32[]{:S(2)}, u32[]{:S(2)}) %collective-permute-start.25) | collective-permute-done | bytes 442400 | tf_op jit(solution)/shard_map/ppermute | solution.py:380
  157.4 0.0 copy-start.2
  157.4 0.0 copy-start.4
  157.4 1.2 collective-permute-start.27
  158.6 2.2 %widen.2.refs_0_ = f32[6912,256]{1,0:T(8,128)} custom-call(s32[1]{0:T(128)} %bitcast.8.half_ref.place_ref, bf16[3456,256]{1,0:T(8,128)(2,1)S(1)} %bitcast.64), custom_call_target="tpu_custom_call" | custom-call | tf_op jit(solution)/shard_map/widen/pallas_call | solution.py:434
  160.8 2.6 %combine.1 = bf16[32,64,256]{2,1,0:T(8,128)(2,1)} custom-call(s32[8,8]{1,0:T(8,128)S(1)} %bitcast.70, f32[32,64,256]{2,1,0:T(8,128)S(1)} %copy-done, bf16[32,64,256]{2,1,0:T(8,128)(2,1)S(1)} %bitcast.68, bf16[8,64,256]{2,1,0:T(8,128)(2,1)S(1)} %collective-permute-done.9.refs_0_, bf16[8,64,256]{2,1,0:T(8,128)(2,1)S(1)} %collective-permute-done.10.refs_1_, ...), custom_call_target="tpu_custom_call" | custom-call | tf_op jit(solution)/shard_map/combine/pallas_call | solution.py:474
  163.5 2.2 %widen.3 = f32[6912,256]{1,0:T(8,128)} custom-call(s32[1]{0:T(128)S(6)} %sub.4.half_ref.place_ref, bf16[3456,256]{1,0:T(8,128)(2,1)S(1)} %collective-permute-done.27.half_ref, f32[6912,256]{1,0:T(8,128)} %widen.2.refs_0_), custom_call_target="tpu_custom_call", output_to_operand_aliasing={{}: (2, {})} | custom-call | tf_op jit(solution)/shard_map/widen/pallas_call | solution.py:434
  (49 shorter events, 0.4 us)
Async XLA Ops:
  0.6 1.2 copy-start.1
  1.9 0.7 copy-start.3
  4.3 12.0 %copy-start.6 = (bf16[8,64,256]{2,1,0:T(8,128)(2,1)}, bf16[8,64,256]{2,1,0:T(8,128)(2,1)S(1)}, u32[]{:S(2)}) copy-start(bf16[8,64,256]{2,1,0:T(8,128)(2,1)S(1)} %get-tuple-element.46) | copy-start | bytes 786436
  4.3 12.0 %copy-start.7 = (bf16[8,64,256]{2,1,0:T(8,128)(2,1)}, bf16[8,64,256]{2,1,0:T(8,128)(2,1)S(1)}, u32[]{:S(2)}) copy-start(bf16[8,64,256]{2,1,0:T(8,128)(2,1)S(1)} %get-tuple-element.45) | copy-start | bytes 786436
  4.3 12.1 %copy-start.8 = (bf16[8,64,256]{2,1,0:T(8,128)(2,1)}, bf16[8,64,256]{2,1,0:T(8,128)(2,1)S(1)}, u32[]{:S(2)}) copy-start(bf16[8,64,256]{2,1,0:T(8,128)(2,1)S(1)} %get-tuple-element.44) | copy-start | bytes 786436
  4.3 15.2 %collective-permute-start = (bf16[8,64,256]{2,1,0:T(8,128)(2,1)}, bf16[8,64,256]{2,1,0:T(8,128)(2,1)}, u32[]{:S(2)}, u32[]{:S(2)}) collective-permute-start(bf16[8,64,256]{2,1,0:T(8,128)(2,1)} %get-tuple-element.39._), channel_id=1, source_target_pairs={{5,0},{6,1},{7,2},{9,4},{10,5},{11,6},{13,8},{14,9},{15,10},{17,12... | collective-permute-start | bytes 786440 | tf_op jit(solution)/shard_map/ppermute | solution.py:43
  5.6 15.3 %collective-permute-start.1 = (bf16[8,64,256]{2,1,0:T(8,128)(2,1)}, bf16[8,64,256]{2,1,0:T(8,128)(2,1)}, u32[]{:S(2)}, u32[]{:S(2)}) collective-permute-start(bf16[8,64,256]{2,1,0:T(8,128)(2,1)} %get-tuple-element.40), channel_id=1, source_target_pairs={{4,0},{5,1},{6,2},{7,3},{8,4},{9,5},{10,6},{11,7},{12,8},{13,9},{1... | collective-permute-start | bytes 786440 | tf_op jit(solution)/shard_map/ppermute | solution.py:43
  6.9 19.3 %collective-permute-start.2 = (bf16[8,64,256]{2,1,0:T(8,128)(2,1)}, bf16[8,64,256]{2,1,0:T(8,128)(2,1)}, u32[]{:S(2)}, u32[]{:S(2)}) collective-permute-start(bf16[8,64,256]{2,1,0:T(8,128)(2,1)} %get-tuple-element.41), channel_id=1, source_target_pairs={{4,1},{5,2},{6,3},{8,5},{9,6},{10,7},{12,9},{13,10},{14,11},{16,13... | collective-permute-start | bytes 786440 | tf_op jit(solution)/shard_map/ppermute | solution.py:43
  8.3 32.7 %collective-permute-start.3 = (bf16[8,64,256]{2,1,0:T(8,128)(2,1)}, bf16[8,64,256]{2,1,0:T(8,128)(2,1)}, u32[]{:S(2)}, u32[]{:S(2)}) collective-permute-start(bf16[8,64,256]{2,1,0:T(8,128)(2,1)} %get-tuple-element.42), channel_id=1, source_target_pairs={{1,0},{2,1},{3,2},{5,4},{6,5},{7,6},{9,8},{10,9},{11,10},{13,12},{... | collective-permute-start | bytes 786440 | tf_op jit(solution)/shard_map/ppermute | solution.py:43
  9.6 31.5 %collective-permute-start.4 = (bf16[8,64,256]{2,1,0:T(8,128)(2,1)}, bf16[8,64,256]{2,1,0:T(8,128)(2,1)}, u32[]{:S(2)}, u32[]{:S(2)}) collective-permute-start(bf16[8,64,256]{2,1,0:T(8,128)(2,1)} %get-tuple-element.43), channel_id=1, source_target_pairs={{0,1},{1,2},{2,3},{4,5},{5,6},{6,7},{8,9},{9,10},{10,11},{12,13},{... | collective-permute-start | bytes 786440 | tf_op jit(solution)/shard_map/ppermute | solution.py:43
  16.4 19.7 %copy-start.5 = (bf16[27,256,256]{2,1,0:T(8,128)(2,1)S(1)}, bf16[27,256,256]{2,1,0:T(8,128)(2,1)}, u32[]{:S(2)}) copy-start(bf16[27,256,256]{2,1,0:T(8,128)(2,1)} %refs_8_.1) | copy-start | bytes 10616836
  19.5 21.6 %collective-permute-start.5 = (bf16[8,64,256]{2,1,0:T(8,128)(2,1)}, bf16[8,64,256]{2,1,0:T(8,128)(2,1)}, u32[]{:S(2)}, u32[]{:S(2)}) collective-permute-start(bf16[8,64,256]{2,1,0:T(8,128)(2,1)} %copy-done.8), channel_id=1, source_target_pairs={{1,4},{2,5},{3,6},{5,8},{6,9},{7,10},{9,12},{10,13},{11,14},{13,16... | collective-permute-start | bytes 786440 | tf_op jit(solution)/shard_map/ppermute | solution.py:43
  20.9 20.2 %collective-permute-start.6 = (bf16[8,64,256]{2,1,0:T(8,128)(2,1)}, bf16[8,64,256]{2,1,0:T(8,128)(2,1)}, u32[]{:S(2)}, u32[]{:S(2)}) collective-permute-start(bf16[8,64,256]{2,1,0:T(8,128)(2,1)} %copy-done.7), channel_id=1, source_target_pairs={{0,4},{1,5},{2,6},{3,7},{4,8},{5,9},{6,10},{7,11},{8,12},{9,13},{1... | collective-permute-start | bytes 786440 | tf_op jit(solution)/shard_map/ppermute | solution.py:43
  26.1 14.9 %collective-permute-start.7 = (bf16[8,64,256]{2,1,0:T(8,128)(2,1)}, bf16[8,64,256]{2,1,0:T(8,128)(2,1)}, u32[]{:S(2)}, u32[]{:S(2)}) collective-permute-start(bf16[8,64,256]{2,1,0:T(8,128)(2,1)} %copy-done.6), channel_id=1, source_target_pairs={{0,5},{1,6},{2,7},{4,9},{5,10},{6,11},{8,13},{9,14},{10,15},{12,17... | collective-permute-start | bytes 786440 | tf_op jit(solution)/shard_map/ppermute | solution.py:43
  36.0 0.7 copy-start.10
  39.2 1.8 %copy-start.9 = (bf16[27,256,256]{2,1,0:T(8,128)(2,1)}, bf16[27,256,256]{2,1,0:T(8,128)(2,1)S(1)}, u32[]{:S(2)}) copy-start(bf16[27,256,256]{2,1,0:T(8,128)(2,1)S(1)} %turn_weights.1.refs_10_.w_hbm) | copy-start | bytes 10616836
  61.8 11.3 %collective-permute-start.8 = (f32[27,128,256]{2,1,0:T(8,128)}, f32[27,128,256]{2,1,0:T(8,128)S(1)}, u32[]{:S(2)}, u32[]{:S(2)}) collective-permute-start(f32[27,128,256]{2,1,0:T(8,128)} %get-tuple-element.51), channel_id=1, source_target_pairs={{0,4},{4,0},{1,5},{5,1},{2,6},{6,2},{3,7},{7,3},{8,12},{12,8},{9,1... | collective-permute-start | bytes 10616840 | tf_op jit(solution)/shard_map/ppermute | solution.py:373
  73.1 25.1 %copy-start.11 = (f32[27,128,256]{2,1,0:T(8,128)}, f32[27,128,256]{2,1,0:T(8,128)S(1)}, u32[]{:S(2)}) copy-start(f32[27,128,256]{2,1,0:T(8,128)S(1)} %collective-permute-done.8) | copy-start | bytes 10616836
  77.4 37.0 %collective-permute-start.11 = (bf16[864,256]{1,0:T(8,128)(2,1)}, bf16[864,256]{1,0:T(8,128)(2,1)}, u32[]{:S(2)}, u32[]{:S(2)}) collective-permute-start(bf16[864,256]{1,0:T(8,128)(2,1)} %get-tuple-element.56), channel_id=1, source_target_pairs={{0,1},{1,2},{2,3},{3,0},{4,5},{5,6},{6,7},{7,4},{8,9},{9,10},{10,1... | collective-permute-start | bytes 1327112 | tf_op jit(solution)/shard_map/ppermute | solution.py:380
  79.7 34.6 %collective-permute-start.12 = (bf16[864,256]{1,0:T(8,128)(2,1)}, bf16[864,256]{1,0:T(8,128)(2,1)}, u32[]{:S(2)}, u32[]{:S(2)}) collective-permute-start(bf16[864,256]{1,0:T(8,128)(2,1)} %get-tuple-element.57), channel_id=1, source_target_pairs={{0,2},{1,3},{2,0},{3,1},{4,6},{5,7},{6,4},{7,5},{8,10},{9,11},{10,... | collective-permute-start | bytes 1327112 | tf_op jit(solution)/shard_map/ppermute | solution.py:380
  80.0 34.3 %collective-permute-start.13 = (bf16[864,256]{1,0:T(8,128)(2,1)}, bf16[864,256]{1,0:T(8,128)(2,1)}, u32[]{:S(2)}, u32[]{:S(2)}) collective-permute-start(bf16[864,256]{1,0:T(8,128)(2,1)} %get-tuple-element.58), channel_id=1, source_target_pairs={{0,3},{1,0},{2,1},{3,2},{4,7},{5,4},{6,5},{7,6},{8,11},{9,8},{10,9... | collective-permute-start | bytes 1327112 | tf_op jit(solution)/shard_map/ppermute | solution.py:380
  98.2 7.0 %collective-permute-start.9 = (bf16[8,64,256]{2,1,0:T(8,128)(2,1)}, bf16[8,64,256]{2,1,0:T(8,128)(2,1)S(1)}, u32[]{:S(2)}, u32[]{:S(2)}) collective-permute-start(bf16[8,64,256]{2,1,0:T(8,128)(2,1)} %get-tuple-element.54), channel_id=1, source_target_pairs={{0,1},{1,2},{2,3},{4,5},{5,6},{6,7},{8,9},{9,10},{10,11},{12,13},{... | collective-permute-start | bytes 786440 | tf_op jit(solution)/shard_map/ppermute | solution.py:43
  99.5 14.8 %collective-permute-start.10 = (bf16[8,64,256]{2,1,0:T(8,128)(2,1)}, bf16[8,64,256]{2,1,0:T(8,128)(2,1)S(1)}, u32[]{:S(2)}, u32[]{:S(2)}) collective-permute-start(bf16[8,64,256]{2,1,0:T(8,128)(2,1)} %get-tuple-element.55), channel_id=1, source_target_pairs={{1,0},{2,1},{3,2},{5,4},{6,5},{7,6},{9,8},{10,9},{11,10},{13,12},{... | collective-permute-start | bytes 786440 | tf_op jit(solution)/shard_map/ppermute | solution.py:43
  105.2 19.0 %copy-start.14 = (bf16[16,64,256]{2,1,0:T(8,128)(2,1)S(1)}, bf16[16,64,256]{2,1,0:T(8,128)(2,1)}, u32[]{:S(2)}) copy-start(bf16[16,64,256]{2,1,0:T(8,128)(2,1)} %get-tuple-element.67) | copy-start | bytes 1572868
  105.2 25.0 %collective-permute-start.14 = (bf16[16,64,256]{2,1,0:T(8,128)(2,1)}, bf16[16,64,256]{2,1,0:T(8,128)(2,1)S(1)}, u32[]{:S(2)}, u32[]{:S(2)}) collective-permute-start(bf16[16,64,256]{2,1,0:T(8,128)(2,1)} %get-tuple-element.62), channel_id=1, source_target_pairs={{0,1},{1,2},{2,3},{4,5},{5,6},{6,7},{8,9},{9,10},{10,11},{12,13},{... | collective-permute-start | bytes 1572872 | tf_op jit(solution)/shard_map/ppermute | solution.py:43
  116.5 9.0 %collective-permute-start.17 = (bf16[216,256]{1,0:T(8,128)(2,1)S(1)}, bf16[216,256]{1,0:T(8,128)(2,1)S(1)}, u32[]{:S(2)}, u32[]{:S(2)}) collective-permute-start(bf16[216,256]{1,0:T(8,128)(2,1)S(1)} %get-tuple-element.79), channel_id=1, source_target_pairs={{0,24},{8,0},{16,8},{24,16},{1,25},{9,1},{17,9},{25,17},{2,26},{10... | collective-permute-start | bytes 331784 | tf_op jit(solution)/shard_map/ppermute | solution.py:380
  120.4 9.8 %collective-permute-start.16 = (bf16[216,256]{1,0:T(8,128)(2,1)S(1)}, bf16[216,256]{1,0:T(8,128)(2,1)S(1)}, u32[]{:S(2)}, u32[]{:S(2)}) collective-permute-start(bf16[216,256]{1,0:T(8,128)(2,1)S(1)} %get-tuple-element.80), channel_id=1, source_target_pairs={{0,16},{8,24},{16,0},{24,8},{1,17},{9,25},{17,1},{25,9},{2,18},{10... | collective-permute-start | bytes 331784 | tf_op jit(solution)/shard_map/ppermute | solution.py:380
  122.6 7.6 %collective-permute-start.15 = (bf16[216,256]{1,0:T(8,128)(2,1)S(1)}, bf16[216,256]{1,0:T(8,128)(2,1)S(1)}, u32[]{:S(2)}, u32[]{:S(2)}) collective-permute-start(bf16[216,256]{1,0:T(8,128)(2,1)S(1)} %get-tuple-element.78), channel_id=1, source_target_pairs={{0,8},{8,16},{16,24},{24,0},{1,9},{9,17},{17,25},{25,1},{2,10},{10... | collective-permute-start | bytes 331784 | tf_op jit(solution)/shard_map/ppermute | solution.py:380
  124.2 16.1 %collective-permute-start.18 = (bf16[16,64,256]{2,1,0:T(8,128)(2,1)S(1)}, bf16[16,64,256]{2,1,0:T(8,128)(2,1)S(1)}, u32[]{:S(2)}, u32[]{:S(2)}) collective-permute-start(bf16[16,64,256]{2,1,0:T(8,128)(2,1)S(1)} %copy-done.14), channel_id=1, source_target_pairs={{1,0},{2,1},{3,2},{5,4},{6,5},{7,6},{9,8},{10,9},{11,10},{13,12},{... | collective-permute-start | bytes 1572872 | tf_op jit(solution)/shard_map/ppermute | solution.py:43
  130.2 13.0 %copy-start.13 = (bf16[8,64,256]{2,1,0:T(8,128)(2,1)S(1)}, bf16[8,64,256]{2,1,0:T(8,128)(2,1)}, u32[]{:S(2)}) copy-start(bf16[8,64,256]{2,1,0:T(8,128)(2,1)} %get-tuple-element.61) | copy-start | bytes 786436
  130.3 6.0 %collective-permute-start.19 = (bf16[216,256]{1,0:T(8,128)(2,1)S(1)}, bf16[216,256]{1,0:T(8,128)(2,1)S(1)}, u32[]{:S(2)}, u32[]{:S(2)}) collective-permute-start(bf16[216,256]{1,0:T(8,128)(2,1)S(1)} %fusion.7), channel_id=1, source_target_pairs={{0,24},{8,0},{16,8},{24,16},{1,25},{9,1},{17,9},{25,17},{2,26},{10... | collective-permute-start | bytes 331784 | tf_op jit(solution)/shard_map/ppermute | solution.py:380
  131.4 8.9 %collective-permute-start.20 = (bf16[216,256]{1,0:T(8,128)(2,1)S(1)}, bf16[216,256]{1,0:T(8,128)(2,1)S(1)}, u32[]{:S(2)}, u32[]{:S(2)}) collective-permute-start(bf16[216,256]{1,0:T(8,128)(2,1)S(1)} %fusion.7), channel_id=1, source_target_pairs={{0,16},{8,24},{16,0},{24,8},{1,17},{9,25},{17,1},{25,9},{2,18},{10... | collective-permute-start | bytes 331784 | tf_op jit(solution)/shard_map/ppermute | solution.py:380
  132.9 7.4 %collective-permute-start.21 = (bf16[216,256]{1,0:T(8,128)(2,1)S(1)}, bf16[216,256]{1,0:T(8,128)(2,1)S(1)}, u32[]{:S(2)}, u32[]{:S(2)}) collective-permute-start(bf16[216,256]{1,0:T(8,128)(2,1)S(1)} %fusion.7), channel_id=1, source_target_pairs={{0,8},{8,16},{16,24},{24,0},{1,9},{9,17},{17,25},{25,1},{2,10},{10... | collective-permute-start | bytes 331784 | tf_op jit(solution)/shard_map/ppermute | solution.py:380
  135.0 9.7 %copy-start.12 = (bf16[8,64,256]{2,1,0:T(8,128)(2,1)S(1)}, bf16[8,64,256]{2,1,0:T(8,128)(2,1)}, u32[]{:S(2)}) copy-start(bf16[8,64,256]{2,1,0:T(8,128)(2,1)} %get-tuple-element.70) | copy-start | bytes 786436
  140.4 12.1 %collective-permute-start.24 = (bf16[864,256]{1,0:T(8,128)(2,1)S(1)}, bf16[864,256]{1,0:T(8,128)(2,1)S(1)}, u32[]{:S(2)}, u32[]{:S(2)}) collective-permute-start(bf16[864,256]{1,0:T(8,128)(2,1)S(1)} %bitcast.78), channel_id=1, source_target_pairs={{0,3},{1,0},{2,1},{3,2},{4,7},{5,4},{6,5},{7,6},{8,11},{9,8},{10,9... | collective-permute-start | bytes 1327112 | tf_op jit(solution)/shard_map/ppermute | solution.py:380
  140.4 16.8 %collective-permute-start.25 = (bf16[864,256]{1,0:T(8,128)(2,1)S(1)}, bf16[864,256]{1,0:T(8,128)(2,1)S(1)}, u32[]{:S(2)}, u32[]{:S(2)}) collective-permute-start(bf16[864,256]{1,0:T(8,128)(2,1)S(1)} %bitcast.79), channel_id=1, source_target_pairs={{0,2},{1,3},{2,0},{3,1},{4,6},{5,7},{6,4},{7,5},{8,10},{9,11},{10,... | collective-permute-start | bytes 1327112 | tf_op jit(solution)/shard_map/ppermute | solution.py:380
  142.2 15.1 %collective-permute-start.26 = (bf16[864,256]{1,0:T(8,128)(2,1)S(1)}, bf16[864,256]{1,0:T(8,128)(2,1)S(1)}, u32[]{:S(2)}, u32[]{:S(2)}) collective-permute-start(bf16[864,256]{1,0:T(8,128)(2,1)S(1)} %bitcast.80), channel_id=1, source_target_pairs={{0,1},{1,2},{2,3},{3,0},{4,5},{5,6},{6,7},{7,4},{8,9},{9,10},{10,1... | collective-permute-start | bytes 1327112 | tf_op jit(solution)/shard_map/ppermute | solution.py:380
  143.3 14.0 %collective-permute-start.22 = (bf16[24,64,256]{2,1,0:T(8,128)(2,1)S(1)}, bf16[24,64,256]{2,1,0:T(8,128)(2,1)S(1)}, u32[]{:S(2)}, u32[]{:S(2)}) collective-permute-start(bf16[24,64,256]{2,1,0:T(8,128)(2,1)S(1)} %pad_maximum_fusion), channel_id=1, source_target_pairs={{0,4},{1,5},{2,6},{3,7},{4,8},{5,9},{6,10},{7,11},{8,12},{9,13},{1... | collective-permute-start | bytes 2359304 | tf_op jit(solution)/shard_map/ppermute | solution.py:43
  144.8 12.6 %collective-permute-start.23 = (bf16[24,64,256]{2,1,0:T(8,128)(2,1)S(1)}, bf16[24,64,256]{2,1,0:T(8,128)(2,1)S(1)}, u32[]{:S(2)}, u32[]{:S(2)}) collective-permute-start(bf16[24,64,256]{2,1,0:T(8,128)(2,1)S(1)} %pad_maximum_fusion.1), channel_id=1, source_target_pairs={{4,0},{5,1},{6,2},{7,3},{8,4},{9,5},{10,6},{11,7},{12,8},{13,9},{1... | collective-permute-start | bytes 2359304 | tf_op jit(solution)/shard_map/ppermute | solution.py:43
  157.4 3.5 %copy-start = (f32[32,64,256]{2,1,0:T(8,128)S(1)}, f32[32,64,256]{2,1,0:T(8,128)}, u32[]{:S(2)}) copy-start(f32[32,64,256]{2,1,0:T(8,128)} %get-tuple-element.53.own_ref) | copy-start | bytes 6291460
  157.4 3.4 %copy-start.2 = (bf16[1,1,32,64,256]{4,3,2,1,0:T(8,128)(2,1)S(1)}, bf16[1,1,32,64,256]{4,3,2,1,0:T(8,128)(2,1)}, u32[]{:S(2)}) copy-start(bf16[1,1,32,64,256]{4,3,2,1,0:T(8,128)(2,1)} %param.10) | copy-start | bytes 3145732
  157.4 3.4 %copy-start.4 = (s32[1,1,8,8]{3,2,1,0:T(8,128)S(1)}, s32[1,1,8,8]{3,2,1,0:T(8,128)}, u32[]{:S(2)}) copy-start(s32[1,1,8,8]{3,2,1,0:T(8,128)} %param.11) | copy-start | bytes 772
  157.4 6.1 %collective-permute-start.27 = (bf16[3456,256]{1,0:T(8,128)(2,1)S(1)}, bf16[3456,256]{1,0:T(8,128)(2,1)S(1)}, u32[]{:S(2)}, u32[]{:S(2)}) collective-permute-start(bf16[3456,256]{1,0:T(8,128)(2,1)S(1)} %bitcast.63), channel_id=1, source_target_pairs={{0,4},{4,0},{1,5},{5,1},{2,6},{6,2},{3,7},{7,3},{8,12},{12,8},{9,1... | collective-permute-start | bytes 5308424 | tf_op jit(solution)/shard_map/ppermute | solution.py:373
where the time goes:
time: 167 us; the launch traced here: 166 us
  starting transfers between devices  61.8 us (37%)
  Pallas kernels  61.7 us (37%)
  waiting for transfers between devices  28.9 us (17%)
  other arithmetic  6.51 us (4%)
  local copies, waits for them, and re-layouts  4.94 us (3%)
  between operations  1.85 us (1%)
    ppermute x14, starting transfers between devices, travel(): return lax.ppermute(packet, ('gz', 'core', 'gy'), pairs)  39.9 us
    ppermute x12, waiting for transfers between devices, move(): return lax.ppermute(x, axis, [(i, (i + by) % size) for i in range(size)])  20.9 us
    pallas_call x1, Pallas kernels, forward_and_terms(): pl.pallas_call(kernel, out_shape=out_shape, in_specs=[SMEM, SMEM, HBM] +...  20.8 us
    ppermute x12, starting transfers between devices, move(): return lax.ppermute(x, axis, [(i, (i + by) % size) for i in range(size)])  20.6 us
    pallas_call x1, Pallas kernels, input_grad(): pl.pallas_call(kernel, out_shape=out_shape, in_specs=[SMEM, HBM, HBM], ou...  15.5 us
    pallas_call x1, Pallas kernels, weight_terms(): pl.pallas_call(kernel, out_shape=out_shape, in_specs=[SMEM, SMEM, HBM, HB...  11.2 us
    ppermute x14, waiting for transfers between devices, travel(): return lax.ppermute(packet, ('gz', 'core', 'gy'), pairs)  7.99 us
    unnamed x30, local copies, waits for them, and re-layouts  4.46 us
  transfers between devices with their start and end apart: 28, of which 7 were waited for; matrix products, arithmetic and copies ran while one was open for 2% of the time, Pallas kernels for 22%

commit v1 on v0

--- a/solution.py
+++ b/solution.py
@@ -142,7 +142,7 @@
     )(after, weights)
 
 
-def forward_and_terms(table, half, tiles, halos, weights, cotangent, scale, after):
+def forward_and_terms(table, half, tiles, order, halos, weights, cotangent, scale, after):
     tile_slots, voxels, channels = tiles.shape
     offset_count = weights.shape[0]
     directions, halo = len(halos), halos[0].shape[0]
@@ -157,7 +157,7 @@
         w_hbm, cot_hbm, _, out_hbm, grad_hbm, turned_hbm, ext_hbm, half_hbm = refs[:8]
         w_ref, cot_ref, out_ref, grad, turned_ref, ext, half_out, acc, sems, w_sems = refs[8:]
         copies = [pltpu.make_async_copy(tiles_ref, ext.at[pl.ds(0, tile_slots)], sems.at[0])]
-        for d, halo_ref in enumerate(halo_refs):
+        for d, halo_ref in zip(order, halo_refs):
             place = ext.at[pl.ds(tile_slots + d * halo, halo)]
             copies.append(pltpu.make_async_copy(halo_ref, place, sems.at[d + 6]))
 
@@ -496,6 +496,11 @@
     core = lax.axis_index("core").astype(jnp.int32)[None]
 
     packets = pack(tiles, lists)
+    order = [
+        DIRECTIONS.index(pair)
+        for pair in ((-1, 0), (1, 0), (-1, -1), (1, 1), (-1, 1), (1, -1), (0, -1), (0, 1))
+    ]
+    arrived = {d: travel(packets[d], *DIRECTIONS[d]) for d in order}
     table = source_table(
         block_offset[0, 0],
         block_input[0, 0].T,
@@ -504,17 +509,12 @@
         offset_count,
         tile_slots,
         tile_slots + directions * halo,
-        packets[0],
+        arrived[order[0]],
     )
     turned_weights = turn_weights(weights, table)
-    order = [
-        DIRECTIONS.index(pair)
-        for pair in ((-1, -1), (1, 1), (-1, 0), (1, 0), (-1, 1), (1, -1), (0, -1), (0, 1))
-    ]
-    arrived = {d: travel(packets[d], *DIRECTIONS[d]) for d in order}
-    halos = [arrived[d] for d in range(directions)]
+    halos = [arrived[d] for d in order]
     out_features, pre_grad, turned, ext, send = forward_and_terms(
-        table, 1 - core, tiles, halos, weights, incoming, scale, turned_weights
+        table, 1 - core, tiles, order, halos, weights, incoming, scale, turned_weights
     )
     received = to_other_core(send)
     keep = weight_terms(table, core, ext, turned, offset_count, scale)

time: 167 us -> 176 us (1.054)
  waiting for transfers between devices: 28.9 us -> 35.9 us
  local copies, waits for them, and re-layouts: 4.94 us -> 7.81 us
    ppermute x12, waiting for transfers between devices: 20.9 us -> 26.2 us  [move(): return lax.ppermute(x, axis, [(i, (i + by) % size) for i in range(size)])]
    unnamed x30 -> x34, local copies, waits for them, and re-layouts: 4.46 us -> 7.33 us
    ppermute x12, starting transfers between devices: 20.6 us -> 22.4 us  [move(): return lax.ppermute(x, axis, [(i, (i + by) % size) for i in range(size)])]
  transfers between devices with their start and end apart: 28 -> 28, of which waited for: 7 -> 9; matrix products, arithmetic and copies ran while one was open for 2% -> 2% of each run, Pallas kernels for 22% -> 21%
where the time goes in v1:
time: 176 us; the launch traced here: 175 us
  Pallas kernels  61.6 us (35%)
  starting transfers between devices  61.2 us (35%)
  waiting for transfers between devices  35.9 us (20%)
  local copies, waits for them, and re-layouts  7.81 us (4%)
  other arithmetic  6.5 us (4%)
  between operations  1.86 us (1%)
    ppermute x14, starting transfers between devices, travel(): return lax.ppermute(packet, ('gz', 'core', 'gy'), pairs)  38.7 us
    ppermute x12, waiting for transfers between devices, move(): return lax.ppermute(x, axis, [(i, (i + by) % size) for i in range(size)])  26.2 us
    ppermute x12, starting transfers between devices, move(): return lax.ppermute(x, axis, [(i, (i + by) % size) for i in range(size)])  22.4 us
    pallas_call x1, Pallas kernels, forward_and_terms(): pl.pallas_call(kernel, out_shape=out_shape, in_specs=[SMEM, SMEM, HBM] +...  20.8 us
    pallas_call x1, Pallas kernels, input_grad(): pl.pallas_call(kernel, out_shape=out_shape, in_specs=[SMEM, HBM, HBM], ou...  15.5 us
    pallas_call x1, Pallas kernels, weight_terms(): pl.pallas_call(kernel, out_shape=out_shape, in_specs=[SMEM, SMEM, HBM, HB...  11.2 us
    ppermute x14, waiting for transfers between devices, travel(): return lax.ppermute(packet, ('gz', 'core', 'gy'), pairs)  9.66 us
    unnamed x34, local copies, waits for them, and re-layouts  7.33 us
  transfers between devices with their start and end apart: 28, of which 9 were waited for; matrix products, arithmetic and copies ran while one was open for 2% of the time, Pallas kernels for 21%

profile of v1, /device:TPU:0, one launch (start us, length us, event | category | flops | bytes accessed | tf_op | source)
XLA Modules:
  0.0 174.9 jit_solution(4810814409332755745)
XLA Ops:
  0.6 1.2 copy-done.1
  1.9 0.7 copy-done.3
  2.5 1.8 %pack.1 = (bf16[8,64,256]{2,1,0:T(8,128)(2,1)}, bf16[8,64,256]{2,1,0:T(8,128)(2,1)S(1)}, bf16[8,64,256]{2,1,0:T(8,128)(2,1)}, bf16[8,64,256]{2,1,0:T(8,128)(2,1)...) custom-call(s32[8,8]{1,0:T(8,128)S(1)} %bitcast.69, ...), custom_call_target="tpu_custom_call" | custom-call | tf_op jit(solution)/shard_map/pack/pallas_call | solution.py:55
  4.3 0.7 copy-done.6
  5.0 0.7 copy-done.7
  5.7 1.3 collective-permute-start
  7.0 3.7 %collective-permute-start.1 = (bf16[8,64,256]{2,1,0:T(8,128)(2,1)}, bf16[8,64,256]{2,1,0:T(8,128)(2,1)}, u32[]{:S(2)}, u32[]{:S(2)}) collective-permute-start(bf16[8,64,256]{2,1,0:T(8,128)(2,1)} %get-tuple-element.40), channel_id=1, source_target_pairs={{0,4},{1,5},{2,6},{3,7},{4,8},{5,9},{6,10},{7,11},{8,12},{9,13},{1... | collective-permute-start | bytes 786440 | tf_op jit(solution)/shard_map/ppermute | solution.py:43
  10.7 1.3 collective-permute-start.2
  12.0 6.3 %collective-permute-start.3 = (bf16[8,64,256]{2,1,0:T(8,128)(2,1)}, bf16[8,64,256]{2,1,0:T(8,128)(2,1)}, u32[]{:S(2)}, u32[]{:S(2)}) collective-permute-start(bf16[8,64,256]{2,1,0:T(8,128)(2,1)} %get-tuple-element.42), channel_id=1, source_target_pairs={{0,5},{1,6},{2,7},{4,9},{5,10},{6,11},{8,13},{9,14},{10,15},{12,17... | collective-permute-start | bytes 786440 | tf_op jit(solution)/shard_map/ppermute | solution.py:43
  18.3 1.4 collective-permute-start.4
  20.4 1.4 collective-permute-start.5
  21.8 3.0 %source_table.1._.table_ref = s32[27,33]{1,0:T(8,128)} custom-call(s32[108]{0:T(128)} %bitcast.85, s32[8,108]{1,0:T(8,128)} %bitcast.83, s32[8,108]{1,0:T(8,128)} %bitcast.84, s32[1]{0:T(128)} %bitcast.62.count_ref, bf16[8,64,256]{2,1,0:T(8,128)(2,1)} %copy-done.14), custom_call_target="tpu_custom_call" | custom-call | flops 4000000000 | bytes 1048576 | tf_op jit(solution)/shard_map/source_table/pallas_call | solution.py:84
  24.8 1.3 collective-permute-start.6
  26.1 9.4 %collective-permute-start.7 = (bf16[8,64,256]{2,1,0:T(8,128)(2,1)}, bf16[8,64,256]{2,1,0:T(8,128)(2,1)S(1)}, u32[]{:S(2)}, u32[]{:S(2)}) collective-permute-start(bf16[8,64,256]{2,1,0:T(8,128)(2,1)} %copy-done.6), channel_id=1, source_target_pairs={{0,1},{1,2},{2,3},{4,5},{5,6},{6,7},{8,9},{9,10},{10,11},{12,13},{... | collective-permute-start | bytes 786440 | tf_op jit(solution)/shard_map/ppermute | solution.py:43
  35.5 0.7 copy-done.9
  36.2 2.5 %turn_weights.1.refs_10_.w_hbm = bf16[27,256,256]{2,1,0:T(8,128)(2,1)S(1)} custom-call(s32[27,33]{1,0:T(8,128)S(1)} %copy-done.9, bf16[27,256,256]{2,1,0:T(8,128)(2,1)S(1)} %copy-done.5), custom_call_target="tpu_custom_call" | custom-call | flops 8000000000 | bytes 7340032 | tf_op jit(solution)/shard_map/turn_weights/pallas_call | solution.py:133
  38.7 0.0 copy-start.8
  38.7 1.8 %copy-done.8 = bf16[27,256,256]{2,1,0:T(8,128)(2,1)} copy-done((bf16[27,256,256]{2,1,0:T(8,128)(2,1)}, bf16[27,256,256]{2,1,0:T(8,128)(2,1)S(1)}, u32[]{:S(2)}) %copy-start.8) | copy-done | bytes 3538968
  40.5 0.2 collective-permute-done.6.refs_6_
  40.7 1.7 collective-permute-done.7.refs_7_
  42.4 0.7 copy-done.16
  43.1 20.8 %forward_and_terms.1 = (bf16[32,64,256]{2,1,0:T(8,128)(2,1)}, bf16[32,64,256]{2,1,0:T(8,128)(2,1)}, bf16[256,2048]{1,0:T(8,128)(2,1)}, bf16[97,64,256]{2,1,0:T(8,128)(2,1)}, f32[27,128,256]{2,1,0:T(8,128)}) custom-call(s32[27,33]{1,0:T(8,128)} %source_table.1._.table_ref, s32[1]{0:T(128)S(6)} %sub.4.half_ref.place_ref, bf16[32,64,256]{2,1,0:T(8,128)(2,1)} %bitcast.65, ...), custom_call_target="tpu_custom_call" | custom-call | flops 10871635968 | bytes 20971520 | tf_op jit(solution)/shard_map/forward_and_terms/pallas_call | solution.py:228
  63.9 0.1 collective-permute-start.8
  64.0 11.2 %weight_terms.1 = f32[27,128,256]{2,1,0:T(8,128)} custom-call(s32[27,33]{1,0:T(8,128)} %source_table.1._.table_ref, s32[1]{0:T(128)} %bitcast.8.half_ref.place_ref, bf16[97,64,256]{2,1,0:T(8,128)(2,1)} %get-tuple-element.49.ext_hbm, bf16[256,2048]{1,0:T(8,128)(2,1)} %get-tuple-element.50.turned_hbm), custom_call_target="tpu_custom_call" | custom-call | flops 3623878656 | bytes 6291456 | tf_op jit(solution)/shard_map/weight_terms/pallas_call | solution.py:266
  75.2 4.2 %fusion.4 = (bf16[864,256]{1,0:T(8,128)(2,1)}, bf16[864,256]{1,0:T(8,128)(2,1)}, bf16[864,256]{1,0:T(8,128)(2,1)}) fusion(f32[4,864,256]{2,1,0:T(8,128)S(1)} %bitcast.72, s32[]{:T(128)S(6)} %select_n.104, f32[4,864,256]{2,1,0:T(8,128)} %bitcast.74, s32[]{:T(128)S(6)} %select_n.102, s32[]{:T(128)S(6)} %select_n.100), kind=kLoop, calls=%fused_computation.10 | loop fusion | flops 1327104 | bytes 6635532 | tf_op jit(solution)/shard_map/convert_element_type | solution.py:396
  79.4 3.8 %collective-permute-start.11 = (bf16[864,256]{1,0:T(8,128)(2,1)}, bf16[864,256]{1,0:T(8,128)(2,1)}, u32[]{:S(2)}, u32[]{:S(2)}) collective-permute-start(bf16[864,256]{1,0:T(8,128)(2,1)} %get-tuple-element.56), channel_id=1, source_target_pairs={{0,1},{1,2},{2,3},{3,0},{4,5},{5,6},{6,7},{7,4},{8,9},{9,10},{10,1... | collective-permute-start | bytes 1327112 | tf_op jit(solution)/shard_map/ppermute | solution.py:380
  83.2 3.5 %collective-permute-start.12 = (bf16[864,256]{1,0:T(8,128)(2,1)}, bf16[864,256]{1,0:T(8,128)(2,1)}, u32[]{:S(2)}, u32[]{:S(2)}) collective-permute-start(bf16[864,256]{1,0:T(8,128)(2,1)} %get-tuple-element.57), channel_id=1, source_target_pairs={{0,2},{1,3},{2,0},{3,1},{4,6},{5,7},{6,4},{7,5},{8,10},{9,11},{10,... | collective-permute-start | bytes 1327112 | tf_op jit(solution)/shard_map/ppermute | solution.py:380
  86.8 1.0 collective-permute-start.13
  87.8 15.5 %input_grad.1 = (f32[32,64,256]{2,1,0:T(8,128)}, bf16[8,64,256]{2,1,0:T(8,128)(2,1)}, bf16[8,64,256]{2,1,0:T(8,128)(2,1)}, bf16[16,64,256]{2,1,0:T(8,128)(2,1)},...) custom-call(s32[27,33]{1,0:T(8,128)} %source_table.1._.table_ref, ...), custom_call_target="tpu_custom_call" | custom-call | flops 7247757312 | bytes 12582912 | tf_op jit(solution)/shard_map/input_grad/pallas_call | solution.py:354
  103.2 2.9 %collective-permute-start.9 = (bf16[8,64,256]{2,1,0:T(8,128)(2,1)}, bf16[8,64,256]{2,1,0:T(8,128)(2,1)S(1)}, u32[]{:S(2)}, u32[]{:S(2)}) collective-permute-start(bf16[8,64,256]{2,1,0:T(8,128)(2,1)} %get-tuple-element.54), channel_id=1, source_target_pairs={{0,1},{1,2},{2,3},{4,5},{5,6},{6,7},{8,9},{9,10},{10,11},{12,13},{... | collective-permute-start | bytes 786440 | tf_op jit(solution)/shard_map/ppermute | solution.py:43
  106.2 1.3 collective-permute-start.10
  107.5 4.3 %collective-permute-done.9.refs_0_ = bf16[8,64,256]{2,1,0:T(8,128)(2,1)S(1)} collective-permute-done((bf16[8,64,256]{2,1,0:T(8,128)(2,1)}, bf16[8,64,256]{2,1,0:T(8,128)(2,1)S(1)}, u32[]{:S(2)}, u32[]{:S(2)}) %collective-permute-start.9) | collective-permute-done | bytes 262176 | tf_op jit(solution)/shard_map/ppermute | solution.py:43
  111.9 4.4 %collective-permute-start.14 = (bf16[16,64,256]{2,1,0:T(8,128)(2,1)}, bf16[16,64,256]{2,1,0:T(8,128)(2,1)S(1)}, u32[]{:S(2)}, u32[]{:S(2)}) collective-permute-start(bf16[16,64,256]{2,1,0:T(8,128)(2,1)} %get-tuple-element.62), channel_id=1, source_target_pairs={{0,1},{1,2},{2,3},{4,5},{5,6},{6,7},{8,9},{9,10},{10,11},{12,13},{... | collective-permute-start | bytes 1572872 | tf_op jit(solution)/shard_map/ppermute | solution.py:43
  116.3 3.4 %collective-permute-done.10.refs_1_ = bf16[8,64,256]{2,1,0:T(8,128)(2,1)S(1)} collective-permute-done((bf16[8,64,256]{2,1,0:T(8,128)(2,1)}, bf16[8,64,256]{2,1,0:T(8,128)(2,1)S(1)}, u32[]{:S(2)}, u32[]{:S(2)}) %collective-permute-start.10) | collective-permute-done | bytes 262176 | tf_op jit(solution)/shard_map/ppermute | solution.py:43
  119.8 2.1 %fusion.1 = f32[864,256]{1,0:T(8,128)S(1)} fusion(bf16[864,256]{1,0:T(8,128)(2,1)} %collective-permute-done.13, bf16[864,256]{1,0:T(8,128)(2,1)} %collective-permute-done.12, bf16[864,256]{1,0:T(8,128)(2,1)} %collective-permute-done.11, f32[4,864,256]{2,1,0:T(8,128)} %bitcast.73, s32[]{:T(128)S(6)} %select_n.106, f32[4,864,256]{2,1,0:T(8,128)} %bitcast.75), kind=kLoop, calls=%fused_computation.2 | loop fusion | flops 1548288 | bytes 3981316 | tf_op jit(solution)/shard_map/add | solution.py:405
  121.8 0.1 fusion.8
  121.9 4.0 %collective-permute-start.17 = (bf16[216,256]{1,0:T(8,128)(2,1)S(1)}, bf16[216,256]{1,0:T(8,128)(2,1)S(1)}, u32[]{:S(2)}, u32[]{:S(2)}) collective-permute-start(bf16[216,256]{1,0:T(8,128)(2,1)S(1)} %get-tuple-element.79), channel_id=1, source_target_pairs={{0,24},{8,0},{16,8},{24,16},{1,25},{9,1},{17,9},{25,17},{2,26},{10... | collective-permute-start | bytes 331784 | tf_op jit(solution)/shard_map/ppermute | solution.py:380
  125.9 3.1 %collective-permute-start.16 = (bf16[216,256]{1,0:T(8,128)(2,1)S(1)}, bf16[216,256]{1,0:T(8,128)(2,1)S(1)}, u32[]{:S(2)}, u32[]{:S(2)}) collective-permute-start(bf16[216,256]{1,0:T(8,128)(2,1)S(1)} %get-tuple-element.80), channel_id=1, source_target_pairs={{0,16},{8,24},{16,0},{24,8},{1,17},{9,25},{17,1},{25,9},{2,18},{10... | collective-permute-start | bytes 331784 | tf_op jit(solution)/shard_map/ppermute | solution.py:380
  128.9 1.6 collective-permute-start.15
  130.6 1.3 collective-permute-start.18
  131.9 5.6 %collective-permute-done.16 = bf16[216,256]{1,0:T(8,128)(2,1)S(1)} collective-permute-done((bf16[216,256]{1,0:T(8,128)(2,1)S(1)}, bf16[216,256]{1,0:T(8,128)(2,1)S(1)}, u32[]{:S(2)}, u32[]{:S(2)}) %collective-permute-start.16) | collective-permute-done | bytes 110624 | tf_op jit(solution)/shard_map/ppermute | solution.py:380
  137.5 0.1 fusion.7
  137.6 0.6 collective-permute-start.19
  138.2 0.7 collective-permute-start.20
  138.8 1.9 %collective-permute-start.21 = (bf16[216,256]{1,0:T(8,128)(2,1)S(1)}, bf16[216,256]{1,0:T(8,128)(2,1)S(1)}, u32[]{:S(2)}, u32[]{:S(2)}) collective-permute-start(bf16[216,256]{1,0:T(8,128)(2,1)S(1)} %fusion.7), channel_id=1, source_target_pairs={{0,8},{8,16},{16,24},{24,0},{1,9},{9,17},{17,25},{25,1},{2,10},{10... | collective-permute-start | bytes 331784 | tf_op jit(solution)/shard_map/ppermute | solution.py:380
  140.9 1.7 collective-permute-done.19
  142.6 5.7 %collective-permute-done.20 = bf16[216,256]{1,0:T(8,128)(2,1)S(1)} collective-permute-done((bf16[216,256]{1,0:T(8,128)(2,1)S(1)}, bf16[216,256]{1,0:T(8,128)(2,1)S(1)}, u32[]{:S(2)}, u32[]{:S(2)}) %collective-permute-start.20) | collective-permute-done | bytes 110624 | tf_op jit(solution)/shard_map/ppermute | solution.py:380
  148.4 0.1 collective-permute-start.24
  148.4 2.1 %collective-permute-start.25 = (bf16[864,256]{1,0:T(8,128)(2,1)S(1)}, bf16[864,256]{1,0:T(8,128)(2,1)S(1)}, u32[]{:S(2)}, u32[]{:S(2)}) collective-permute-start(bf16[864,256]{1,0:T(8,128)(2,1)S(1)} %bitcast.79), channel_id=1, source_target_pairs={{0,2},{1,3},{2,0},{3,1},{4,6},{5,7},{6,4},{7,5},{8,10},{9,11},{10,... | collective-permute-start | bytes 1327112 | tf_op jit(solution)/shard_map/ppermute | solution.py:380
  150.6 0.1 pad_maximum_fusion
  150.7 1.3 collective-permute-start.22
  152.1 0.1 pad_maximum_fusion.1
  152.2 1.3 collective-permute-start.23
  153.5 0.1 broadcast_in_dim.48
  153.6 7.9 %collective-permute-done.24 = bf16[864,256]{1,0:T(8,128)(2,1)S(1)} collective-permute-done((bf16[864,256]{1,0:T(8,128)(2,1)S(1)}, bf16[864,256]{1,0:T(8,128)(2,1)S(1)}, u32[]{:S(2)}, u32[]{:S(2)}) %collective-permute-start.24) | collective-permute-done | bytes 442400 | tf_op jit(solution)/shard_map/ppermute | solution.py:380
  161.6 5.3 %collective-permute-done.25 = bf16[864,256]{1,0:T(8,128)(2,1)S(1)} collective-permute-done((bf16[864,256]{1,0:T(8,128)(2,1)S(1)}, bf16[864,256]{1,0:T(8,128)(2,1)S(1)}, u32[]{:S(2)}, u32[]{:S(2)}) %collective-permute-start.25) | collective-permute-done | bytes 442400 | tf_op jit(solution)/shard_map/ppermute | solution.py:380
  167.0 0.0 copy-start.2
  167.0 0.0 copy-start.4
  167.0 0.1 collective-permute-start.27
  167.1 2.2 %widen.2.refs_0_ = f32[6912,256]{1,0:T(8,128)} custom-call(s32[1]{0:T(128)} %bitcast.8.half_ref.place_ref, bf16[3456,256]{1,0:T(8,128)(2,1)S(1)} %bitcast.64), custom_call_target="tpu_custom_call" | custom-call | tf_op jit(solution)/shard_map/widen/pallas_call | solution.py:434
  169.3 0.2 copy-done
  169.5 0.6 copy-done.2
  170.1 2.6 %combine.1 = bf16[32,64,256]{2,1,0:T(8,128)(2,1)} custom-call(s32[8,8]{1,0:T(8,128)S(1)} %bitcast.70, f32[32,64,256]{2,1,0:T(8,128)S(1)} %copy-done, bf16[32,64,256]{2,1,0:T(8,128)(2,1)S(1)} %bitcast.68, bf16[8,64,256]{2,1,0:T(8,128)(2,1)S(1)} %collective-permute-done.9.refs_0_, bf16[8,64,256]{2,1,0:T(8,128)(2,1)S(1)} %collective-permute-done.10.refs_1_, ...), custom_call_target="tpu_custom_call" | custom-call | tf_op jit(solution)/shard_map/combine/pallas_call | solution.py:474
  172.8 2.2 %widen.3 = f32[6912,256]{1,0:T(8,128)} custom-call(s32[1]{0:T(128)S(6)} %sub.4.half_ref.place_ref, bf16[3456,256]{1,0:T(8,128)(2,1)S(1)} %collective-permute-done.27.half_ref, f32[6912,256]{1,0:T(8,128)} %widen.2.refs_0_), custom_call_target="tpu_custom_call", output_to_operand_aliasing={{}: (2, {})} | custom-call | tf_op jit(solution)/shard_map/widen/pallas_call | solution.py:434
  (53 shorter events, 0.4 us)
Async XLA Ops:
  0.6 1.2 copy-start.1
  1.9 0.7 copy-start.3
  4.3 0.7 copy-start.6
  5.0 0.7 copy-start.7
  5.7 14.7 %collective-permute-start = (bf16[8,64,256]{2,1,0:T(8,128)(2,1)S(1)}, bf16[8,64,256]{2,1,0:T(8,128)(2,1)S(1)}, u32[]{:S(2)}, u32[]{:S(2)}) collective-permute-start(bf16[8,64,256]{2,1,0:T(8,128)(2,1)S(1)} %get-tuple-element.39), channel_id=1, source_target_pairs={{4,0},{5,1},{6,2},{7,3},{8,4},{9,5},{10,6},{11,7},{12,8},{13,9},{1... | collective-permute-start | bytes 786440 | tf_op jit(solution)/shard_map/ppermute | solution.py:43
  7.0 17.8 %collective-permute-start.1 = (bf16[8,64,256]{2,1,0:T(8,128)(2,1)}, bf16[8,64,256]{2,1,0:T(8,128)(2,1)}, u32[]{:S(2)}, u32[]{:S(2)}) collective-permute-start(bf16[8,64,256]{2,1,0:T(8,128)(2,1)} %get-tuple-element.40), channel_id=1, source_target_pairs={{0,4},{1,5},{2,6},{3,7},{4,8},{5,9},{6,10},{7,11},{8,12},{9,13},{1... | collective-permute-start | bytes 786440 | tf_op jit(solution)/shard_map/ppermute | solution.py:43
  10.7 15.4 %collective-permute-start.2 = (bf16[8,64,256]{2,1,0:T(8,128)(2,1)}, bf16[8,64,256]{2,1,0:T(8,128)(2,1)}, u32[]{:S(2)}, u32[]{:S(2)}) collective-permute-start(bf16[8,64,256]{2,1,0:T(8,128)(2,1)} %get-tuple-element.41), channel_id=1, source_target_pairs={{5,0},{6,1},{7,2},{9,4},{10,5},{11,6},{13,8},{14,9},{15,10},{17,12... | collective-permute-start | bytes 786440 | tf_op jit(solution)/shard_map/ppermute | solution.py:43
  12.0 28.5 %collective-permute-start.3 = (bf16[8,64,256]{2,1,0:T(8,128)(2,1)}, bf16[8,64,256]{2,1,0:T(8,128)(2,1)}, u32[]{:S(2)}, u32[]{:S(2)}) collective-permute-start(bf16[8,64,256]{2,1,0:T(8,128)(2,1)} %get-tuple-element.42), channel_id=1, source_target_pairs={{0,5},{1,6},{2,7},{4,9},{5,10},{6,11},{8,13},{9,14},{10,15},{12,17... | collective-permute-start | bytes 786440 | tf_op jit(solution)/shard_map/ppermute | solution.py:43
  18.3 22.2 %collective-permute-start.4 = (bf16[8,64,256]{2,1,0:T(8,128)(2,1)}, bf16[8,64,256]{2,1,0:T(8,128)(2,1)}, u32[]{:S(2)}, u32[]{:S(2)}) collective-permute-start(bf16[8,64,256]{2,1,0:T(8,128)(2,1)} %get-tuple-element.43), channel_id=1, source_target_pairs={{4,1},{5,2},{6,3},{8,5},{9,6},{10,7},{12,9},{13,10},{14,11},{16,13... | collective-permute-start | bytes 786440 | tf_op jit(solution)/shard_map/ppermute | solution.py:43
  20.4 1.4 copy-start.14
  20.4 20.2 %collective-permute-start.5 = (bf16[8,64,256]{2,1,0:T(8,128)(2,1)}, bf16[8,64,256]{2,1,0:T(8,128)(2,1)}, u32[]{:S(2)}, u32[]{:S(2)}) collective-permute-start(bf16[8,64,256]{2,1,0:T(8,128)(2,1)} %get-tuple-element.44), channel_id=1, source_target_pairs={{1,4},{2,5},{3,6},{5,8},{6,9},{7,10},{9,12},{10,13},{11,14},{13,16... | collective-permute-start | bytes 786440 | tf_op jit(solution)/shard_map/ppermute | solution.py:43
  21.8 13.8 %copy-start.5 = (bf16[27,256,256]{2,1,0:T(8,128)(2,1)S(1)}, bf16[27,256,256]{2,1,0:T(8,128)(2,1)}, u32[]{:S(2)}) copy-start(bf16[27,256,256]{2,1,0:T(8,128)(2,1)} %refs_8_.1) | copy-start | bytes 10616836
  24.8 16.0 %collective-permute-start.6 = (bf16[8,64,256]{2,1,0:T(8,128)(2,1)}, bf16[8,64,256]{2,1,0:T(8,128)(2,1)S(1)}, u32[]{:S(2)}, u32[]{:S(2)}) collective-permute-start(bf16[8,64,256]{2,1,0:T(8,128)(2,1)} %copy-done.7), channel_id=1, source_target_pairs={{1,0},{2,1},{3,2},{5,4},{6,5},{7,6},{9,8},{10,9},{11,10},{13,12},{... | collective-permute-start | bytes 786440 | tf_op jit(solution)/shard_map/ppermute | solution.py:43
  26.1 16.3 %collective-permute-start.7 = (bf16[8,64,256]{2,1,0:T(8,128)(2,1)}, bf16[8,64,256]{2,1,0:T(8,128)(2,1)S(1)}, u32[]{:S(2)}, u32[]{:S(2)}) collective-permute-start(bf16[8,64,256]{2,1,0:T(8,128)(2,1)} %copy-done.6), channel_id=1, source_target_pairs={{0,1},{1,2},{2,3},{4,5},{5,6},{6,7},{8,9},{9,10},{10,11},{12,13},{... | collective-permute-start | bytes 786440 | tf_op jit(solution)/shard_map/ppermute | solution.py:43
  35.5 0.7 copy-start.9
  38.7 1.8 %copy-start.8 = (bf16[27,256,256]{2,1,0:T(8,128)(2,1)}, bf16[27,256,256]{2,1,0:T(8,128)(2,1)S(1)}, u32[]{:S(2)}) copy-start(bf16[27,256,256]{2,1,0:T(8,128)(2,1)S(1)} %turn_weights.1.refs_10_.w_hbm) | copy-start | bytes 10616836
  40.7 1.7 copy-start.15
  42.4 0.7 copy-start.16
  63.9 11.3 %collective-permute-start.8 = (f32[27,128,256]{2,1,0:T(8,128)}, f32[27,128,256]{2,1,0:T(8,128)S(1)}, u32[]{:S(2)}, u32[]{:S(2)}) collective-permute-start(f32[27,128,256]{2,1,0:T(8,128)} %get-tuple-element.51), channel_id=1, source_target_pairs={{0,4},{4,0},{1,5},{5,1},{2,6},{6,2},{3,7},{7,3},{8,12},{12,8},{9,1... | collective-permute-start | bytes 10616840 | tf_op jit(solution)/shard_map/ppermute | solution.py:373
  75.2 28.1 %copy-start.10 = (f32[27,128,256]{2,1,0:T(8,128)}, f32[27,128,256]{2,1,0:T(8,128)S(1)}, u32[]{:S(2)}) copy-start(f32[27,128,256]{2,1,0:T(8,128)S(1)} %collective-permute-done.8) | copy-start | bytes 10616836
  79.4 40.4 %collective-permute-start.11 = (bf16[864,256]{1,0:T(8,128)(2,1)}, bf16[864,256]{1,0:T(8,128)(2,1)}, u32[]{:S(2)}, u32[]{:S(2)}) collective-permute-start(bf16[864,256]{1,0:T(8,128)(2,1)} %get-tuple-element.56), channel_id=1, source_target_pairs={{0,1},{1,2},{2,3},{3,0},{4,5},{5,6},{6,7},{7,4},{8,9},{9,10},{10,1... | collective-permute-start | bytes 1327112 | tf_op jit(solution)/shard_map/ppermute | solution.py:380
  83.2 36.5 %collective-permute-start.12 = (bf16[864,256]{1,0:T(8,128)(2,1)}, bf16[864,256]{1,0:T(8,128)(2,1)}, u32[]{:S(2)}, u32[]{:S(2)}) collective-permute-start(bf16[864,256]{1,0:T(8,128)(2,1)} %get-tuple-element.57), channel_id=1, source_target_pairs={{0,2},{1,3},{2,0},{3,1},{4,6},{5,7},{6,4},{7,5},{8,10},{9,11},{10,... | collective-permute-start | bytes 1327112 | tf_op jit(solution)/shard_map/ppermute | solution.py:380
  86.8 33.0 %collective-permute-start.13 = (bf16[864,256]{1,0:T(8,128)(2,1)}, bf16[864,256]{1,0:T(8,128)(2,1)}, u32[]{:S(2)}, u32[]{:S(2)}) collective-permute-start(bf16[864,256]{1,0:T(8,128)(2,1)} %get-tuple-element.58), channel_id=1, source_target_pairs={{0,3},{1,0},{2,1},{3,2},{4,7},{5,4},{6,5},{7,6},{8,11},{9,8},{10,9... | collective-permute-start | bytes 1327112 | tf_op jit(solution)/shard_map/ppermute | solution.py:380
  103.2 8.6 %collective-permute-start.9 = (bf16[8,64,256]{2,1,0:T(8,128)(2,1)}, bf16[8,64,256]{2,1,0:T(8,128)(2,1)S(1)}, u32[]{:S(2)}, u32[]{:S(2)}) collective-permute-start(bf16[8,64,256]{2,1,0:T(8,128)(2,1)} %get-tuple-element.54), channel_id=1, source_target_pairs={{0,1},{1,2},{2,3},{4,5},{5,6},{6,7},{8,9},{9,10},{10,11},{12,13},{... | collective-permute-start | bytes 786440 | tf_op jit(solution)/shard_map/ppermute | solution.py:43
  106.2 13.6 %collective-permute-start.10 = (bf16[8,64,256]{2,1,0:T(8,128)(2,1)}, bf16[8,64,256]{2,1,0:T(8,128)(2,1)S(1)}, u32[]{:S(2)}, u32[]{:S(2)}) collective-permute-start(bf16[8,64,256]{2,1,0:T(8,128)(2,1)} %get-tuple-element.55), channel_id=1, source_target_pairs={{1,0},{2,1},{3,2},{5,4},{6,5},{7,6},{9,8},{10,9},{11,10},{13,12},{... | collective-permute-start | bytes 786440 | tf_op jit(solution)/shard_map/ppermute | solution.py:43
  111.9 18.7 %copy-start.13 = (bf16[16,64,256]{2,1,0:T(8,128)(2,1)S(1)}, bf16[16,64,256]{2,1,0:T(8,128)(2,1)}, u32[]{:S(2)}) copy-start(bf16[16,64,256]{2,1,0:T(8,128)(2,1)} %get-tuple-element.67) | copy-start | bytes 1572868
  111.9 25.7 %collective-permute-start.14 = (bf16[16,64,256]{2,1,0:T(8,128)(2,1)}, bf16[16,64,256]{2,1,0:T(8,128)(2,1)S(1)}, u32[]{:S(2)}, u32[]{:S(2)}) collective-permute-start(bf16[16,64,256]{2,1,0:T(8,128)(2,1)} %get-tuple-element.62), channel_id=1, source_target_pairs={{0,1},{1,2},{2,3},{4,5},{5,6},{6,7},{8,9},{9,10},{10,11},{12,13},{... | collective-permute-start | bytes 1572872 | tf_op jit(solution)/shard_map/ppermute | solution.py:43
  121.9 10.0 %collective-permute-start.17 = (bf16[216,256]{1,0:T(8,128)(2,1)S(1)}, bf16[216,256]{1,0:T(8,128)(2,1)S(1)}, u32[]{:S(2)}, u32[]{:S(2)}) collective-permute-start(bf16[216,256]{1,0:T(8,128)(2,1)S(1)} %get-tuple-element.79), channel_id=1, source_target_pairs={{0,24},{8,0},{16,8},{24,16},{1,25},{9,1},{17,9},{25,17},{2,26},{10... | collective-permute-start | bytes 331784 | tf_op jit(solution)/shard_map/ppermute | solution.py:380
  125.9 11.6 %collective-permute-start.16 = (bf16[216,256]{1,0:T(8,128)(2,1)S(1)}, bf16[216,256]{1,0:T(8,128)(2,1)S(1)}, u32[]{:S(2)}, u32[]{:S(2)}) collective-permute-start(bf16[216,256]{1,0:T(8,128)(2,1)S(1)} %get-tuple-element.80), channel_id=1, source_target_pairs={{0,16},{8,24},{16,0},{24,8},{1,17},{9,25},{17,1},{25,9},{2,18},{10... | collective-permute-start | bytes 331784 | tf_op jit(solution)/shard_map/ppermute | solution.py:380
  128.9 8.6 %collective-permute-start.15 = (bf16[216,256]{1,0:T(8,128)(2,1)S(1)}, bf16[216,256]{1,0:T(8,128)(2,1)S(1)}, u32[]{:S(2)}, u32[]{:S(2)}) collective-permute-start(bf16[216,256]{1,0:T(8,128)(2,1)S(1)} %get-tuple-element.78), channel_id=1, source_target_pairs={{0,8},{8,16},{16,24},{24,0},{1,9},{9,17},{17,25},{25,1},{2,10},{10... | collective-permute-start | bytes 331784 | tf_op jit(solution)/shard_map/ppermute | solution.py:380
  130.6 17.8 %collective-permute-start.18 = (bf16[16,64,256]{2,1,0:T(8,128)(2,1)S(1)}, bf16[16,64,256]{2,1,0:T(8,128)(2,1)S(1)}, u32[]{:S(2)}, u32[]{:S(2)}) collective-permute-start(bf16[16,64,256]{2,1,0:T(8,128)(2,1)S(1)} %copy-done.13), channel_id=1, source_target_pairs={{1,0},{2,1},{3,2},{5,4},{6,5},{7,6},{9,8},{10,9},{11,10},{13,12},{... | collective-permute-start | bytes 1572872 | tf_op jit(solution)/shard_map/ppermute | solution.py:43
  137.5 13.1 %copy-start.12 = (bf16[8,64,256]{2,1,0:T(8,128)(2,1)S(1)}, bf16[8,64,256]{2,1,0:T(8,128)(2,1)}, u32[]{:S(2)}) copy-start(bf16[8,64,256]{2,1,0:T(8,128)(2,1)} %get-tuple-element.61) | copy-start | bytes 786436
  137.6 5.0 %collective-permute-start.19 = (bf16[216,256]{1,0:T(8,128)(2,1)S(1)}, bf16[216,256]{1,0:T(8,128)(2,1)S(1)}, u32[]{:S(2)}, u32[]{:S(2)}) collective-permute-start(bf16[216,256]{1,0:T(8,128)(2,1)S(1)} %fusion.7), channel_id=1, source_target_pairs={{0,24},{8,0},{16,8},{24,16},{1,25},{9,1},{17,9},{25,17},{2,26},{10... | collective-permute-start | bytes 331784 | tf_op jit(solution)/shard_map/ppermute | solution.py:380
  138.2 10.2 %collective-permute-start.20 = (bf16[216,256]{1,0:T(8,128)(2,1)S(1)}, bf16[216,256]{1,0:T(8,128)(2,1)S(1)}, u32[]{:S(2)}, u32[]{:S(2)}) collective-permute-start(bf16[216,256]{1,0:T(8,128)(2,1)S(1)} %fusion.7), channel_id=1, source_target_pairs={{0,16},{8,24},{16,0},{24,8},{1,17},{9,25},{17,1},{25,9},{2,18},{10... | collective-permute-start | bytes 331784 | tf_op jit(solution)/shard_map/ppermute | solution.py:380
  138.8 9.5 %collective-permute-start.21 = (bf16[216,256]{1,0:T(8,128)(2,1)S(1)}, bf16[216,256]{1,0:T(8,128)(2,1)S(1)}, u32[]{:S(2)}, u32[]{:S(2)}) collective-permute-start(bf16[216,256]{1,0:T(8,128)(2,1)S(1)} %fusion.7), channel_id=1, source_target_pairs={{0,8},{8,16},{16,24},{24,0},{1,9},{9,17},{17,25},{25,1},{2,10},{10... | collective-permute-start | bytes 331784 | tf_op jit(solution)/shard_map/ppermute | solution.py:380
  140.9 11.2 %copy-start.11 = (bf16[8,64,256]{2,1,0:T(8,128)(2,1)S(1)}, bf16[8,64,256]{2,1,0:T(8,128)(2,1)}, u32[]{:S(2)}) copy-start(bf16[8,64,256]{2,1,0:T(8,128)(2,1)} %get-tuple-element.70) | copy-start | bytes 786436
  148.4 13.2 %collective-permute-start.24 = (bf16[864,256]{1,0:T(8,128)(2,1)S(1)}, bf16[864,256]{1,0:T(8,128)(2,1)S(1)}, u32[]{:S(2)}, u32[]{:S(2)}) collective-permute-start(bf16[864,256]{1,0:T(8,128)(2,1)S(1)} %bitcast.78), channel_id=1, source_target_pairs={{0,3},{1,0},{2,1},{3,2},{4,7},{5,4},{6,5},{7,6},{8,11},{9,8},{10,9... | collective-permute-start | bytes 1327112 | tf_op jit(solution)/shard_map/ppermute | solution.py:380
  148.4 18.4 %collective-permute-start.25 = (bf16[864,256]{1,0:T(8,128)(2,1)S(1)}, bf16[864,256]{1,0:T(8,128)(2,1)S(1)}, u32[]{:S(2)}, u32[]{:S(2)}) collective-permute-start(bf16[864,256]{1,0:T(8,128)(2,1)S(1)} %bitcast.79), channel_id=1, source_target_pairs={{0,2},{1,3},{2,0},{3,1},{4,6},{5,7},{6,4},{7,5},{8,10},{9,11},{10,... | collective-permute-start | bytes 1327112 | tf_op jit(solution)/shard_map/ppermute | solution.py:380
  150.6 16.3 %collective-permute-start.26 = (bf16[864,256]{1,0:T(8,128)(2,1)S(1)}, bf16[864,256]{1,0:T(8,128)(2,1)S(1)}, u32[]{:S(2)}, u32[]{:S(2)}) collective-permute-start(bf16[864,256]{1,0:T(8,128)(2,1)S(1)} %bitcast.80), channel_id=1, source_target_pairs={{0,1},{1,2},{2,3},{3,0},{4,5},{5,6},{6,7},{7,4},{8,9},{9,10},{10,1... | collective-permute-start | bytes 1327112 | tf_op jit(solution)/shard_map/ppermute | solution.py:380
  150.7 16.2 %collective-permute-start.22 = (bf16[24,64,256]{2,1,0:T(8,128)(2,1)S(1)}, bf16[24,64,256]{2,1,0:T(8,128)(2,1)S(1)}, u32[]{:S(2)}, u32[]{:S(2)}) collective-permute-start(bf16[24,64,256]{2,1,0:T(8,128)(2,1)S(1)} %pad_maximum_fusion), channel_id=1, source_target_pairs={{0,4},{1,5},{2,6},{3,7},{4,8},{5,9},{6,10},{7,11},{8,12},{9,13},{1... | collective-permute-start | bytes 2359304 | tf_op jit(solution)/shard_map/ppermute | solution.py:43
  152.2 14.8 %collective-permute-start.23 = (bf16[24,64,256]{2,1,0:T(8,128)(2,1)S(1)}, bf16[24,64,256]{2,1,0:T(8,128)(2,1)S(1)}, u32[]{:S(2)}, u32[]{:S(2)}) collective-permute-start(bf16[24,64,256]{2,1,0:T(8,128)(2,1)S(1)} %pad_maximum_fusion.1), channel_id=1, source_target_pairs={{4,0},{5,1},{6,2},{7,3},{8,4},{9,5},{10,6},{11,7},{12,8},{13,9},{1... | collective-permute-start | bytes 2359304 | tf_op jit(solution)/shard_map/ppermute | solution.py:43
  167.0 2.6 %copy-start = (f32[32,64,256]{2,1,0:T(8,128)S(1)}, f32[32,64,256]{2,1,0:T(8,128)}, u32[]{:S(2)}) copy-start(f32[32,64,256]{2,1,0:T(8,128)} %get-tuple-element.53.own_ref) | copy-start | bytes 6291460
  167.0 3.1 %copy-start.2 = (bf16[1,1,32,64,256]{4,3,2,1,0:T(8,128)(2,1)S(1)}, bf16[1,1,32,64,256]{4,3,2,1,0:T(8,128)(2,1)}, u32[]{:S(2)}) copy-start(bf16[1,1,32,64,256]{4,3,2,1,0:T(8,128)(2,1)} %param.10) | copy-start | bytes 3145732
  167.0 3.1 %copy-start.4 = (s32[1,1,8,8]{3,2,1,0:T(8,128)S(1)}, s32[1,1,8,8]{3,2,1,0:T(8,128)}, u32[]{:S(2)}) copy-start(s32[1,1,8,8]{3,2,1,0:T(8,128)} %param.11) | copy-start | bytes 772
  167.0 5.7 %collective-permute-start.27 = (bf16[3456,256]{1,0:T(8,128)(2,1)S(1)}, bf16[3456,256]{1,0:T(8,128)(2,1)S(1)}, u32[]{:S(2)}, u32[]{:S(2)}) collective-permute-start(bf16[3456,256]{1,0:T(8,128)(2,1)S(1)} %bitcast.63), channel_id=1, source_target_pairs={{0,4},{4,0},{1,5},{5,1},{2,6},{6,2},{3,7},{7,3},{8,12},{12,8},{9,1... | collective-permute-start | bytes 5308424 | tf_op jit(solution)/shard_map/ppermute | solution.py:373
